TPU v7x, 32 devices: a whole 2x2x4 slice. The times are simulated.
32 devices in a mesh: grp: 2 (over core), pen: 4 (over z), blk: 4 (over y, x).
Axes of the slice: x: 2, y: 2, z: 4, core: 2. Of those that a mesh axis runs over, the one named last changes fastest.
Arguments:
- tile_blocks: bfloat16 [1024, 128, 128], P(('grp', 'pen', 'blk')), may hold values from -0.19921875 to 0.19921875
- tile_aux: int32 [1024], P(('grp', 'pen', 'blk')), may hold values from 0 to 31, as said below
- tile_pair: int32 [1024], P(('grp', 'pen', 'blk')), may hold values from 0 to 127
- tile_count: int32 [32], P(('grp', 'pen', 'blk')), may hold values from 4 to 32, as said below
- density: bfloat16 [128, 128], P('blk'), may hold values from -6 to 6
- metric_inv: float32 [32, 128, 128], P('pen'), may hold values from -0.5 to 0.5
- orbitals: bfloat16 [8, 192, 36864], P(None, 'pen'), may hold values from -6 to 6
- pair_index: int32 [16, 2], P(('grp', 'blk')), may hold values from 0 to 7, as said below
Outputs:
- coulomb: float32 [128, 128], P(('grp', 'pen', 'blk'))
- pair_terms: float32 [16, 192, 36864], P(('grp', 'blk'), 'pen')
Inputs may be any that keep to these rules, and one draw needn't show every extreme that they name: `tile_aux`: the auxiliary block of a slot is one of the 8 blocks a * 8 to a * 8 + 7 where a is the pen index of the device holding the slot (slots laid out over grp, pen, blk, slowest first, 32 a device); padding slots hold such indices too. Device d uses the first tile_count[d] of its 32 slots; the rest is padding with arbitrary contents; some device uses all 32 slots. `pair_index`: each row names two different orbitals.
All inputs are finite; a program needn't handle non-finite values.
Results may differ from a plain program's by a relative error of at most 0.0029.
Values may be sent and summed in bfloat16 or wider, within the bound.
No kernel may reach another device: no remote copies, remote signals or barrier semaphores. Data moves between devices by JAX's collectives and lax.ppermute only.
A program may use at most 320 MiB of HBM per device.

v0:
```python
import math

import jax
import jax.numpy as jnp
from jax import lax
from jax.sharding import PartitionSpec as P

NG = 192


PRECISE = lax.Precision.HIGHEST
SPACING = 0.1348


def signed_freq(position, length):
    return jnp.where(position < length // 2, position, position - length)


def coulomb_kernel(square_sum, length):
    box_length = SPACING * length
    kernel_scale = box_length * box_length / math.pi
    squares = square_sum.astype(jnp.float32)
    magnitude = jnp.sqrt(squares)
    denominator = jnp.where(square_sum == 0, 1.0, squares)
    regular = kernel_scale * (1.0 - jnp.cos(math.pi * magnitude)) / denominator
    return jnp.where(square_sum == 0, kernel_scale * math.pi * math.pi / 2.0, regular)


def phase_tables(length, freq_count):
    positions = jnp.arange(length, dtype=jnp.int32)[:, None]
    frequency = jnp.arange(freq_count, dtype=jnp.int32)[None, :]
    angles = (positions * frequency % length).astype(jnp.float32) * (2.0 * math.pi / length)
    return (jnp.cos(angles), jnp.sin(angles))


def combine(cos_part, sin_part, width, forward):
    real_cos = cos_part[..., :width]
    imag_cos = cos_part[..., width:]
    real_sin = sin_part[..., :width]
    imag_sin = sin_part[..., width:]
    if forward:
        return jnp.concatenate([real_cos + imag_sin, imag_cos - real_sin], axis=-1)
    return jnp.concatenate([real_cos - imag_sin, imag_cos + real_sin], axis=-1)


def transform_rows(field_data, cosine, sine, width, forward):
    cos_part = jnp.einsum("pxyk,xv->pvyk", field_data, cosine, precision=PRECISE)
    sin_part = jnp.einsum("pxyk,xv->pvyk", field_data, sine, precision=PRECISE)
    return combine(cos_part, sin_part, width, forward)


def transform_cols(field_data, cosine, sine, width, forward):
    cos_part = jnp.einsum("pxyk,yv->pxvk", field_data, cosine, precision=PRECISE)
    sin_part = jnp.einsum("pxyk,yv->pxvk", field_data, sine, precision=PRECISE)
    return combine(cos_part, sin_part, width, forward)


def tile_pass(tile_blocks, aux_local, pair_ids, live_count, contribute, initial):
    step_rows = 8

    def add_block(step_index, running):
        first_slot = step_index * step_rows
        tile_block = lax.dynamic_slice_in_dim(tile_blocks, first_slot, step_rows, 0)
        aux_block = lax.dynamic_slice_in_dim(aux_local, first_slot, step_rows, 0)
        pair_block = lax.dynamic_slice_in_dim(pair_ids, first_slot, step_rows, 0)
        slot_ids = first_slot + jnp.arange(step_rows, dtype=jnp.int32)
        live_mask = (slot_ids < live_count).astype(jnp.float32)
        return contribute(running, tile_block, aux_block, pair_block, live_mask)

    block_count = (live_count + step_rows - 1) // step_rows
    return lax.fori_loop(0, block_count, add_block, initial)


def body(tile_blocks, tile_aux, tile_pair, tile_count, density, metric_inv, orbitals, pair_index):
    aux_count = metric_inv.shape[0]
    dens_all = lax.all_gather(density, "blk", axis=0, tiled=True)
    aux_local = tile_aux - lax.axis_index("pen") * aux_count
    live_count = tile_count[0]
    work_list = (tile_blocks, aux_local, tile_pair, live_count)
    aux_ids = jnp.arange(aux_count, dtype=jnp.int32)

    def add_fit(running, tile_block, aux_block, pair_block, live_mask):
        dens_rows = dens_all[pair_block]
        partial_value = jnp.einsum(
            "tap,tp->ta", tile_block, dens_rows, preferred_element_type=jnp.float32
        )
        partial_value = partial_value * live_mask[:, None]
        selector = (aux_block[:, None] == aux_ids[None, :]).astype(jnp.float32)
        return running + jnp.einsum("tk,ta->ka", selector, partial_value, precision=PRECISE)

    gamma = jnp.zeros((aux_count, tile_blocks.shape[1]), jnp.float32)
    blocks_in, aux_in, pair_in, count_in = work_list
    gamma = tile_pass(blocks_in, aux_in, pair_in, count_in, add_fit, gamma)
    gamma_all = lax.psum(gamma, ("grp", "blk"))
    coef = jnp.einsum("kab,kb->ka", metric_inv, gamma_all, precision=PRECISE).astype(jnp.bfloat16)

    def add_coulomb(running, tile_block, aux_block, pair_block, live_mask):
        selector = (aux_block[:, None] == aux_ids[None, :]).astype(jnp.bfloat16)
        coef_rows = jnp.dot(selector, coef, preferred_element_type=jnp.float32).astype(jnp.bfloat16)
        partial_value = jnp.einsum(
            "tap,ta->tp", tile_block, coef_rows, preferred_element_type=jnp.float32
        )
        partial_value = partial_value * live_mask[:, None]
        return running.at[pair_block].add(partial_value)

    coulomb_part = jnp.zeros((dens_all.shape[0], tile_blocks.shape[2]), jnp.float32)
    blocks_in, aux_in, pair_in, count_in = work_list
    coulomb_part = tile_pass(blocks_in, aux_in, pair_in, count_in, add_coulomb, coulomb_part)
    coulomb = lax.psum_scatter(coulomb_part, ("grp", "pen", "blk"), scatter_dimension=0, tiled=True)
    grid_size = NG
    plane_rows = orbitals.shape[1]
    orbital_grid = orbitals.reshape(orbitals.shape[0], plane_rows, grid_size, grid_size)
    slab_cols = grid_size // lax.axis_size("pen")
    freq_weight = jnp.ones((grid_size,), jnp.float32)
    depth_cos, depth_sin = phase_tables(grid_size, grid_size)
    forward_depth = jnp.concatenate([depth_cos, -depth_sin], axis=1)
    inverse_depth = jnp.concatenate(
        [depth_cos.T * freq_weight[:, None], -depth_sin.T * freq_weight[:, None]], axis=0
    ) / float(grid_size * grid_size * grid_size)
    grid_cos, grid_sin = phase_tables(grid_size, grid_size)
    left_orbital = orbital_grid[pair_index[:, 0]]
    right_orbital = orbital_grid[pair_index[:, 1]].astype(jnp.float32)
    pair_density = left_orbital.astype(jnp.float32) * right_orbital
    freq_data = jnp.einsum("pxyz,zk->pxyk", pair_density, forward_depth, precision=PRECISE)
    freq_data = transform_cols(freq_data, grid_cos, grid_sin, grid_size, True)
    row_ids = signed_freq(jnp.arange(grid_size, dtype=jnp.int32), grid_size)
    col_ids = signed_freq(
        lax.axis_index("pen") * slab_cols + jnp.arange(slab_cols, dtype=jnp.int32), grid_size
    )
    depth_ids = signed_freq(jnp.arange(grid_size, dtype=jnp.int32), grid_size)
    square_sum = (
        row_ids[:, None, None] * row_ids[:, None, None]
        + col_ids[None, :, None] * col_ids[None, :, None]
        + depth_ids[None, None, :] * depth_ids[None, None, :]
    )
    kernel_grid = coulomb_kernel(square_sum, grid_size)
    kernel_both = jnp.concatenate([kernel_grid, kernel_grid], axis=-1)
    spectral = (
        transform_rows(
            lax.all_to_all(freq_data, "pen", split_axis=2, concat_axis=1, tiled=True),
            grid_cos,
            grid_sin,
            grid_size,
            True,
        )
        * kernel_both[None]
    )
    spatial = transform_rows(spectral, grid_cos, grid_sin, grid_size, False)
    back_data = lax.all_to_all(spatial, "pen", split_axis=1, concat_axis=2, tiled=True)
    back_data = transform_cols(back_data, grid_cos, grid_sin, grid_size, False)
    potential = jnp.einsum("pxyk,kz->pxyz", back_data, inverse_depth, precision=PRECISE)
    pair_terms = potential * right_orbital
    return (coulomb, pair_terms.reshape(pair_terms.shape[0], plane_rows, grid_size * grid_size))


def solution(mesh):
    placed = (
        P(("grp", "pen", "blk"), None, None),
        P(("grp", "pen", "blk")),
        P(("grp", "pen", "blk")),
        P(("grp", "pen", "blk")),
        P("blk", None),
        P("pen", None, None),
        P(None, "pen", None),
        P(("grp", "blk"), None),
    )
    return jax.shard_map(
        body,
        mesh=mesh,
        in_specs=placed,
        out_specs=(P(("grp", "pen", "blk"), None), P(("grp", "blk"), "pen", None)),
        check_vma=False,
    )
```

profile of v0, /device:TPU:8, one launch (start us, length us, event | category | flops | bytes accessed | tf_op | source)
XLA Modules:
  0.0 2141.2 jit_solution(7754028686383450700)
XLA Ops:
  7.2 57.1 %reshape.88 = bf16[8,48,192,192]{3,2,1,0:T(8,128)(2,1)} reshape(bf16[8,48,36864]{2,1,0:T(8,128)(2,1)} %param.18) | data formatting | bytes 56623104 | tf_op jit(solution)/shard_map/reshape | solution.py:112
  138.7 35.9 %fusion.24 = f32[2,48,192,384]{3,2,1,0:T(8,128)} fusion(bf16[2,48,64,192]{3,2,1,0:T(8,128)(2,1)} %gather_fusion.1, bf16[2,48,128,192]{3,2,1,0:T(8,128)(2,1)} %get-tuple-element.107, bf16[2,48,64,192]{3,2,1,0:T(8,128)(2,1)} %gather_fusion.2, bf16[2,48,128,192]{3,2,1,0:T(8,128)(2,1)} %get-tuple-element.115, f32[192,192]{0,1:T(8,128)S(1)} %get-tuple-element.217, ...), kind=kOutput, calls=%fused_computation.44 | convolution fusion | flops 16339378176 | bytes 42762240 | tf_op jit(solution)/shard_map/pxyz,zk->pxyk/dot_general | solution.py:124
  174.6 34.6 %convolution_bitcast_fusion.6 = f32[2,48,192,384]{3,2,1,0:T(8,128)} fusion(f32[2,48,192,384]{3,2,1,0:T(8,128)} %fusion.24), kind=kOutput, calls=%fused_computation.60 | convolution fusion | flops 16307785728 | bytes 56623104 | tf_op jit(solution)/shard_map/pxyk,yv->pxvk/dot_general | solution.py:54
  209.2 34.7 %convolution_bitcast_fusion.7 = f32[2,48,192,384]{3,2,1,0:T(8,128)} fusion(f32[2,48,192,384]{3,2,1,0:T(8,128)} %fusion.24), kind=kOutput, calls=%fused_computation.61 | convolution fusion | flops 16307785728 | bytes 56623104 | tf_op jit(solution)/shard_map/pxyk,yv->pxvk/dot_general | solution.py:53
  243.9 37.7 %slice_add_fusion.3 = (f32[2,48,192,192]{3,2,1,0:T(8,128)}, f32[2,48,192,192]{3,2,1,0:T(8,128)}) fusion(f32[2,48,192,384]{3,2,1,0:T(8,128)} %convolution_bitcast_fusion.6, f32[2,48,192,384]{3,2,1,0:T(8,128)} %convolution_bitcast_fusion.7), kind=kLoop, calls=%fused_computation.52 | loop fusion | flops 7077888 | bytes 84934656 | tf_op jit(solution)/shard_map/add | solution.py:42
  281.6 25.3 %pad_maximum_fusion = f32[2,48,192,384]{3,2,1,0:T(8,128)} fusion(f32[2,48,192,192]{3,2,1,0:T(8,128)} %get-tuple-element.209, f32[2,48,192,192]{3,2,1,0:T(8,128)} %get-tuple-element.208), kind=kLoop, calls=%fused_computation.35 | loop fusion | flops 7077888 | bytes 56623104 | tf_op jit(solution)/shard_map/concatenate | solution.py:42
  306.9 24.6 %copy.41 = f32[2,48,192,384]{3,1,0,2:T(8,128)} copy(f32[2,48,192,384]{3,2,1,0:T(8,128)} %pad_maximum_fusion) | data formatting | bytes 56623104 | tf_op jit(solution)/shard_map/concatenate | solution.py:42
  342.1 36.0 %fusion.30 = f32[192,48,192]{2,0,1:T(8,128)S(1)} fusion(s32[192]{0:T(256)S(1)} %fusion.84, s32[192,48]{0,1:T(8,128)S(1)} %broadcast_add_fusion), kind=kLoop, calls=%fused_computation.69 | loop fusion | flops 15925248 | bytes 7115520 | tf_op jit(solution)/shard_map/jit(_where)/select_n | solution.py:26
  384.8 562.9 %all-to-all-done = f32[2,48,192,384]{3,1,0,2:T(8,128)} async-done(((f32[2,48,192,384]{3,1,0,2:T(8,128)}), f32[2,48,192,384]{3,1,0,2:T(8,128)}, u32[]{:S(2)}, u32[]{:S(2)}) %all-to-all-start) | async-done | bytes 28311584 | tf_op jit(solution)/shard_map/all_to_all | solution.py:140
  947.7 21.0 copy.42
  968.7 34.5 %convolution_bitcast_fusion.4 = f32[2,192,48,384]{3,1,2,0:T(8,128)} fusion(f32[2,192,48,384]{3,1,2,0:T(8,128)} %bitcast.113), kind=kOutput, calls=%fused_computation.58 | convolution fusion | flops 16307785728 | bytes 56623104 | tf_op jit(solution)/shard_map/pxyk,xv->pvyk/dot_general | solution.py:48
  1003.3 34.6 %convolution_bitcast_fusion.5 = f32[2,192,48,384]{3,1,2,0:T(8,128)} fusion(f32[2,192,48,384]{3,1,2,0:T(8,128)} %bitcast.114), kind=kOutput, calls=%fused_computation.59 | convolution fusion | flops 16307785728 | bytes 56623104 | tf_op jit(solution)/shard_map/pxyk,xv->pvyk/dot_general | solution.py:47
  1037.8 37.8 %slice_add_fusion.2 = (f32[2,192,48,192]{3,1,2,0:T(8,128)}, f32[2,192,48,192]{3,1,2,0:T(8,128)}) fusion(f32[2,192,48,384]{3,1,2,0:T(8,128)} %convolution_bitcast_fusion.4, f32[2,192,48,384]{3,1,2,0:T(8,128)} %convolution_bitcast_fusion.5), kind=kLoop, calls=%fused_computation.50 | loop fusion | flops 7077888 | bytes 84934656 | tf_op jit(solution)/shard_map/add | solution.py:42
  1075.6 36.3 %convolution_bitcast_fusion.3 = f32[2,192,48,384]{3,1,2,0:T(8,128)} fusion(f32[2,192,48,192]{3,1,2,0:T(8,128)} %get-tuple-element.207, f32[2,192,48,192]{3,1,2,0:T(8,128)} %get-tuple-element.206, f32[192,48,384]{2,0,1:T(8,128)} %pad_maximum_fusion.2, f32[192,192,1,1]{0,1,3,2:T(8,128)S(1)} %fusion.137), kind=kOutput, calls=%fused_computation.57 | convolution fusion | flops 16321609728 | bytes 70926336 | tf_op jit(solution)/shard_map/pxyk,xv->pvyk/dot_general | solution.py:47
  1111.9 36.0 %convolution_bitcast_fusion.2 = f32[2,192,48,384]{3,1,2,0:T(8,128)} fusion(f32[2,192,48,192]{3,1,2,0:T(8,128)} %get-tuple-element.207, f32[2,192,48,192]{3,1,2,0:T(8,128)} %get-tuple-element.206, f32[192,48,384]{2,0,1:T(8,128)} %pad_maximum_fusion.2, f32[192,192,1,1]{0,1,3,2:T(8,128)S(1)} %fusion.135), kind=kOutput, calls=%fused_computation.56 | convolution fusion | flops 16321609728 | bytes 70926336 | tf_op jit(solution)/shard_map/pxyk,xv->pvyk/dot_general | solution.py:48
  1147.9 37.8 %slice_subtract_fusion.1 = (f32[2,192,48,192]{3,1,2,0:T(8,128)}, f32[2,192,48,192]{3,1,2,0:T(8,128)}) fusion(f32[2,192,48,384]{3,1,2,0:T(8,128)} %convolution_bitcast_fusion.2, f32[2,192,48,384]{3,1,2,0:T(8,128)} %convolution_bitcast_fusion.3), kind=kLoop, calls=%fused_computation.48 | loop fusion | flops 7077888 | bytes 84934656 | tf_op jit(solution)/shard_map/sub | solution.py:43
  1185.7 25.3 %pad_maximum_fusion.1 = f32[2,192,48,384]{3,1,2,0:T(8,128)} fusion(f32[2,192,48,192]{3,1,2,0:T(8,128)} %get-tuple-element.205, f32[2,192,48,192]{3,1,2,0:T(8,128)} %get-tuple-element.204), kind=kLoop, calls=%fused_computation.37 | loop fusion | flops 7077888 | bytes 56623104 | tf_op jit(solution)/shard_map/concatenate | solution.py:43
  1211.0 24.6 %copy.43 = f32[2,192,48,384]{3,2,0,1:T(8,128)} copy(f32[2,192,48,384]{3,1,2,0:T(8,128)} %pad_maximum_fusion.1) | data formatting | bytes 56623104 | tf_op jit(solution)/shard_map/concatenate | solution.py:43
  1287.6 661.6 %all-reduce.3.cloned.1.call-done = f32[128,128]{1,0:T(8,128)} async-done(((f32[128,128]{1,0:T(8,128)}), f32[128,128]{1,0:T(8,128)}) %all-reduce.3.cloned.1.call-update) | async-done | bytes 65552
  1950.5 21.0 copy.44
  1971.5 34.5 %convolution_bitcast_fusion = f32[2,48,192,384]{3,2,1,0:T(8,128)} fusion(f32[2,48,192,384]{3,2,1,0:T(8,128)} %bitcast.115), kind=kOutput, calls=%fused_computation.54 | convolution fusion | flops 16307785728 | bytes 56623104 | tf_op jit(solution)/shard_map/pxyk,yv->pxvk/dot_general | solution.py:54
  2006.0 34.8 %convolution_bitcast_fusion.1 = f32[2,48,192,384]{3,2,1,0:T(8,128)} fusion(f32[2,48,192,384]{3,2,1,0:T(8,128)} %bitcast.116), kind=kOutput, calls=%fused_computation.55 | convolution fusion | flops 16307785728 | bytes 56623104 | tf_op jit(solution)/shard_map/pxyk,yv->pxvk/dot_general | solution.py:53
  2040.8 38.0 %slice_subtract_fusion = (f32[2,48,192,192]{3,2,1,0:T(8,128)}, f32[2,48,192,192]{3,2,1,0:T(8,128)}) fusion(f32[2,48,192,384]{3,2,1,0:T(8,128)} %convolution_bitcast_fusion, f32[2,48,192,384]{3,2,1,0:T(8,128)} %convolution_bitcast_fusion.1), kind=kLoop, calls=%fused_computation.46 | loop fusion | flops 7077888 | bytes 84934656 | tf_op jit(solution)/shard_map/sub | solution.py:43
  2078.8 37.2 %convert_multiply_fusion = f32[2,48,192,192]{3,2,1,0:T(8,128)} fusion(f32[2,48,192,192]{3,2,1,0:T(8,128)} %get-tuple-element.203, f32[2,48,192,192]{3,2,1,0:T(8,128)} %get-tuple-element.202, bf16[2,48,64,192]{3,2,1,0:T(8,128)(2,1)} %gather_fusion.2, bf16[2,48,128,192]{3,2,1,0:T(8,128)(2,1)} %get-tuple-element.115, f32[192,192]{0,1:T(8,128)S(1)} %copy-done.5, ...), kind=kOutput, calls=%fused_computation.42 | convolution fusion | flops 16332374016 | bytes 49840128 | tf_op jit(solution)/shard_map/pxyk,kz->pxyz/dot_general | solution.py:151
  (120 shorter events, 198.1 us)
Async XLA Ops:
  7.2 1271.0 %copy-start = (f32[8,128,128]{2,1,0:T(8,128)S(1)}, f32[8,128,128]{2,1,0:T(8,128)}, u32[]{:S(2)}) copy-start(f32[8,128,128]{2,1,0:T(8,128)} %param.17) | copy-start | bytes 1572868
  85.2 11.6 copy-start.8
  96.8 41.9 %copy-start.2 = (f32[192,192]{0,1:T(8,128)}, f32[192,192]{0,1:T(8,128)S(1)}, u32[]{:S(2)}) copy-start(f32[192,192]{0,1:T(8,128)S(1)} %get-tuple-element.216) | copy-start | bytes 442372
  96.8 41.9 %copy-start.4 = (f32[192,192]{0,1:T(8,128)}, f32[192,192]{0,1:T(8,128)S(1)}, u32[]{:S(2)}) copy-start(f32[192,192]{0,1:T(8,128)S(1)} %get-tuple-element.217) | copy-start | bytes 442372
  331.5 616.2 %all-to-all-start = ((f32[2,48,192,384]{3,1,0,2:T(8,128)}), f32[2,48,192,384]{3,1,0,2:T(8,128)}, u32[]{:S(2)}, u32[]{:S(2)}) async-start(f32[2,48,192,384]{3,1,0,2:T(8,128)} %copy.41), calls=%async_computation | async-start | bytes 56623104 | tf_op jit(solution)/shard_map/all_to_all | solution.py:140
  1235.6 13.1 copy-start.7
  1235.6 21.5 %copy-start.9 = (s32[32]{0:T(128)S(1)}, s32[32]{0:T(128)}, u32[]{:S(2)}) copy-start(s32[32]{0:T(128)} %param.13) | copy-start | bytes 388
  1235.6 21.6 %copy-start.1 = (bf16[32,128,128]{2,1,0:T(8,128)(2,1)S(1)}, bf16[32,128,128]{2,1,0:T(8,128)(2,1)}, u32[]{:S(2)}) copy-start(bf16[32,128,128]{2,1,0:T(8,128)(2,1)} %param.12) | copy-start | bytes 3145732
  1235.6 21.6 %copy-start.10 = (s32[32]{0:T(128)S(1)}, s32[32]{0:T(128)}, u32[]{:S(2)}) copy-start(s32[32]{0:T(128)} %param.14) | copy-start | bytes 388
  1235.6 714.9 %all-to-all-start.1 = ((f32[2,192,48,384]{3,2,0,1:T(8,128)}), f32[2,192,48,384]{3,2,0,1:T(8,128)}, u32[]{:S(2)}, u32[]{:S(2)}) async-start(f32[2,192,48,384]{3,2,0,1:T(8,128)} %copy.43), calls=%async_computation.1 | async-start | bytes 56623104 | tf_op jit(solution)/shard_map/all_to_all | solution.py:149
  1248.0 701.2 %all-reduce.3.cloned.1.call-start = ((), (), s32[]{:S(2)}) async-start(), calls=%async_computation.2 | async-start | bytes 131072
  1286.9 0.6 copy-start.6
  2040.8 38.0 %copy-start.3 = (f32[192,192]{0,1:T(8,128)S(1)}, f32[192,192]{0,1:T(8,128)}, u32[]{:S(2)}) copy-start(f32[192,192]{0,1:T(8,128)} %copy-done.2) | copy-start | bytes 442372
  2040.8 38.0 %copy-start.5 = (f32[192,192]{0,1:T(8,128)S(1)}, f32[192,192]{0,1:T(8,128)}, u32[]{:S(2)}) copy-start(f32[192,192]{0,1:T(8,128)} %copy-done.4) | copy-start | bytes 442372
Sparse Core Ops, SparseCore 0:
  1287.7 661.4 all-reduce.2
where the time goes:
time: 2150 us; the launch traced here: 2140 us
  waiting for transfers between devices  1220 us (57%)
  matrix products  357 us (17%)
  other arithmetic  256 us (12%)
  local copies, waits for them, and re-layouts  245 us (11%)
  blocking collectives  21.8 us (1%)
    unnamed x2, waiting for transfers between devices  662 us
    all_to_all x1, waiting for transfers between devices, body(): lax.all_to_all(freq_data, 'pen', split_axis=2, concat_axis=1, tiled=True)  563 us
    sub x2, other arithmetic, combine(): return jnp.concatenate([real_cos - imag_sin, imag_cos + real_sin], axis=-1)  75.8 us
    add x2, other arithmetic, combine(): return jnp.concatenate([real_cos + imag_sin, imag_cos - real_sin], axis=-1)  75.5 us
    dot_general x2, matrix products, transform_rows(): jnp.einsum('pxyk,xv->pvyk', field_data, cosine, precision=PRECISE)  70.9 us
    dot_general x2, matrix products, transform_rows(): sin_part = jnp.einsum('pxyk,xv->pvyk', field_data, sine, precision=PRECISE)  70.5 us
    dot_general x2, matrix products, transform_cols(): jnp.einsum('pxyk,yv->pxvk', field_data, cosine, precision=PRECISE)  69.5 us
    dot_general x2, matrix products, transform_cols(): sin_part = jnp.einsum('pxyk,yv->pxvk', field_data, sine, precision=PRECISE)  69.2 us
  transfers between devices with their start and end apart: 3, of which 2 were waited for; matrix products, arithmetic and copies ran while one was open for 3% of the time, Pallas kernels for 0%

commit v1 on v0

v1 whole, which is shorter than its diff:
```python
import functools
import math

import jax
import jax.numpy as jnp
import ml_dtypes
import numpy as np
from jax import lax
from jax.experimental import pallas as pl
from jax.experimental.pallas import tpu as pltpu
from jax.sharding import PartitionSpec as P

NG = 192
LANE = 128
TAIL = NG - LANE
PAIR_LANES = 2 * NG
ROWS = 16
NEAR = 2

PRECISE = lax.Precision.HIGHEST
SPACING = 0.1348
VMEM_BYTES = 56 * 1024 * 1024


def signed_freq(position, length):
    return jnp.where(position < length // 2, position, position - length)


def coulomb_kernel(square_sum, length):
    box_length = SPACING * length
    kernel_scale = box_length * box_length / math.pi
    squares = square_sum.astype(jnp.float32)
    magnitude = jnp.sqrt(squares)
    denominator = jnp.where(square_sum == 0, 1.0, squares)
    regular = kernel_scale * (1.0 - jnp.cos(math.pi * magnitude)) / denominator
    return jnp.where(square_sum == 0, kernel_scale * math.pi * math.pi / 2.0, regular)


def cas_table(left, right):
    angles = (left * right % NG) * (2.0 * math.pi / NG)
    return np.cos(angles) + np.sin(angles)


def split_table(table):
    high = table.astype(ml_dtypes.bfloat16)
    return high, (table - high.astype(np.float64)).astype(ml_dtypes.bfloat16)


def split(values):
    high = values.astype(jnp.bfloat16)
    low = (values - high.astype(jnp.float32)).astype(jnp.bfloat16)
    return high, low


def split_rest(values):
    high = values.astype(jnp.bfloat16).astype(jnp.float32)
    return high, values - high


def width_of(slab):
    return slab * NG


def dot32(left, right):
    return jnp.dot(left, right, preferred_element_type=jnp.float32)


def split_dot(values, high_weight, low_weight):
    high, low = split(values)
    return dot32(high, high_weight) + dot32(high, low_weight) + dot32(low, high_weight)


def stacked_dot(stacked, values):
    count = stacked.shape[0] // 2
    high, low = split(values)
    both = dot32(stacked, high)
    return both[:count] + both[count:] + dot32(stacked[:count], low)


def stacked_dot_exact(stacked, values):
    count = stacked.shape[0] // 2
    both = dot32(stacked, values)
    return both[:count] + both[count:]


def forward_kernel(slab, pen, meta_ref, left_ref, right_ref, depth_ref, cols_ref, *refs):
    outs, (rows_ref, head_ref, tail_ref, rest_ref) = refs[-4 - pen : -4], refs[-4:]
    half = NG // 2
    chunk = 32

    def depth_step(step, carry):
        start = pl.multiple_of(step * (chunk * PAIR_LANES), LANE)
        lanes = pl.ds(start, chunk * PAIR_LANES)
        field = left_ref[0, :, lanes].astype(jnp.float32) * right_ref[0, :, lanes].astype(jnp.float32)
        high, low = split(field)
        for parity in range(2):
            parts = []
            for source in (high, low):
                first = parity * LANE
                parts.append(
                    jnp.concatenate(
                        [source[:, k * PAIR_LANES + first : k * PAIR_LANES + first + 2 * LANE] for k in range(chunk)], axis=0
                    )
                )
            table_high, table_low = depth_ref[parity, 0], depth_ref[parity, 1]
            result = dot32(parts[0], table_high) + dot32(parts[0], table_low) + dot32(parts[1], table_high)
            place = pl.ds(pl.multiple_of((parity * half + step * chunk) * ROWS, ROWS), chunk * ROWS)
            rows_ref[0, place, :] = result[:, :LANE]
            rows_ref[1, place, :] = result[:, LANE:]
        return carry

    lax.fori_loop(0, half // chunk, depth_step, 0)
    low_lanes = lax.broadcasted_iota(jnp.int32, (slab // 2, LANE), 1) < TAIL

    @pl.when(pl.program_id(0) == 0)
    def _():
        rest_ref[...] = jnp.zeros_like(rest_ref)

    def rounded(values, place):
        values = values + rest_ref[place, :]
        kept = values.astype(jnp.bfloat16).astype(jnp.float32)
        rest_ref[place, :] = values - kept
        return kept

    def cols_step(plane, carry):
        strided = pl.ds(plane, NG, stride=ROWS)
        field = jnp.concatenate([rows_ref[0, strided, :], rows_ref[1, strided, :]], axis=1)
        result = stacked_dot(cols_ref[...], field)
        head_ref[strided, :] = rounded(result[:, :LANE], pl.ds(0, NG))
        tails = []
        for q in range(pen):
            first = result[q * slab : q * slab + slab // 2, LANE:]
            second = result[q * slab + slab // 2 : (q + 1) * slab, LANE:]
            tails.append(jnp.where(low_lanes, first, second))
        tail_ref[pl.ds(plane, half, stride=ROWS), :] = rounded(jnp.concatenate(tails, axis=0), pl.ds(NG, half))
        return carry

    lax.fori_loop(0, ROWS, cols_step, 0, unroll=4)
    for s in range(pen):
        owner = meta_ref[2] ^ s
        for r in range(slab):
            place = pl.ds(pl.multiple_of((owner * slab + r) * ROWS, ROWS), ROWS)
            outs[s][:, r * LANE : (r + 1) * LANE] = head_ref[place, :].astype(jnp.bfloat16)
        for r in range(slab // 2):
            place = pl.ds(pl.multiple_of((owner * (slab // 2) + r) * ROWS, ROWS), ROWS)
            outs[s][:, (slab + r) * LANE : (slab + r + 1) * LANE] = tail_ref[place, :].astype(jnp.bfloat16)


def middle_kernel(pen, in_pieces, out_pieces, extra, meta_ref, table_ref, grid_ref, part_ref, *refs):
    fields, outs, planes_ref = refs[: len(in_pieces)], refs[len(in_pieces) : -1], refs[-1]
    slab = NG // pen
    block = planes_ref.shape[1]

    def place(s, first, count):
        return pl.ds(pl.multiple_of((meta_ref[2] ^ s) * slab + first, ROWS), count)

    for field, piece in zip(fields, in_pieces):
        planes_ref[place(*piece), :] = field[...]
    spectral = stacked_dot_exact(table_ref[...], planes_ref[...]) * grid_ref[...]
    planes_ref[...] = stacked_dot(table_ref[...], spectral).astype(jnp.bfloat16)
    for out_ref, piece in zip(outs, out_pieces):
        values = planes_ref[place(*piece), :]
        if not (extra and piece[1] + piece[2] == slab):
            out_ref[...] = values
            continue
        lanes = pl.ds(pl.multiple_of(pl.program_id(0) * block, LANE), block)
        out_ref[:, lanes] = values
        high, rest = split_rest(part_ref[meta_ref[2] ^ piece[0]])
        middle, rest = split_rest(rest)
        blank = jnp.zeros((ROWS - 3 * high.shape[0], LANE), jnp.float32)
        if piece[2] > ROWS:
            out_ref[: piece[2] - ROWS, width_of(slab) :] = jnp.zeros((piece[2] - ROWS, LANE), jnp.bfloat16)
        tag = jnp.concatenate([high, middle, rest, blank], axis=0).astype(jnp.bfloat16)
        out_ref[piece[2] - ROWS :, width_of(slab) :] = tag


def inverse_kernel(slab, pen, extra, meta_ref, *refs):
    fields = refs[:pen]
    right_ref, cols_ref, depth_ref = refs[pen : pen + 3]
    out_ref, rows_ref, head_ref, tail_ref = refs[-4:]
    if extra:
        part_ref, out_ref = refs[-4], refs[-5]
        rows = part_ref.shape[0]
        tags = [field[:, width_of(slab) :].astype(jnp.float32) for field in fields]
        part_ref[...] = sum(tag[c * rows : (c + 1) * rows] for c in (2, 1, 0) for tag in tags)
    half = NG // 2
    chunk = 32
    for s in range(pen):
        owner = meta_ref[2] ^ s
        for r in range(slab):
            place = pl.ds(pl.multiple_of((owner * slab + r) * ROWS, ROWS), ROWS)
            head_ref[place, :] = fields[s][:, r * LANE : (r + 1) * LANE].astype(jnp.float32)
        for r in range(slab // 2):
            place = pl.ds(pl.multiple_of((owner * (slab // 2) + r) * ROWS, ROWS), ROWS)
            tail_ref[place, :] = fields[s][:, (slab + r) * LANE : (slab + r + 1) * LANE].astype(jnp.float32)
    low_lanes = lax.broadcasted_iota(jnp.int32, (slab // 2, LANE), 1) < TAIL

    def cols_step(plane, carry):
        strided = pl.ds(plane, NG, stride=ROWS)
        tail = tail_ref[pl.ds(plane, half, stride=ROWS), :]
        pieces = []
        for q in range(pen):
            both = tail[q * (slab // 2) : (q + 1) * (slab // 2)]
            pieces.append(jnp.where(low_lanes, both, 0.0))
            pieces.append(jnp.where(low_lanes, 0.0, both))
        field = jnp.concatenate([head_ref[strided, :], jnp.concatenate(pieces, axis=0)], axis=1)
        result = stacked_dot_exact(cols_ref[...], field.astype(jnp.bfloat16))
        rows_ref[0, strided, :] = result[:, :LANE]
        rows_ref[1, strided, :] = result[:, LANE:]
        return carry

    lax.fori_loop(0, ROWS, cols_step, 0, unroll=4)

    def depth_step(step, carry):
        results = []
        for parity in range(2):
            place = pl.ds(pl.multiple_of((parity * half + step * chunk) * ROWS, ROWS), chunk * ROWS)
            field = jnp.concatenate([rows_ref[0, place, :], rows_ref[1, place, :]], axis=1)
            results.append(split_dot(field, depth_ref[parity, 0], depth_ref[parity, 1]))
        for k in range(chunk):
            even, odd = (value[k * ROWS : (k + 1) * ROWS] for value in results)
            potential = jnp.concatenate([even[:, :LANE], even[:, LANE:] + odd[:, :LANE], odd[:, LANE:]], axis=1)
            lanes = pl.ds(pl.multiple_of((step * chunk + k) * PAIR_LANES, LANE), PAIR_LANES)
            out_ref[0, :, lanes] = potential * right_ref[0, :, lanes].astype(jnp.float32)
        return carry

    lax.fori_loop(0, half // chunk, depth_step, 0)


def whole_spec(shape):
    return pl.BlockSpec(shape, lambda *_: (0,) * len(shape))


def column_scratch():
    return [
        pltpu.VMEM((2, NG * ROWS, LANE), jnp.float32),
        pltpu.VMEM((NG * ROWS, LANE), jnp.float32),
        pltpu.VMEM((NG // 2 * ROWS, LANE), jnp.float32),
    ]


def forward_planes(meta, orbitals, depth_tables, cols_table, pen, first, count, earlier, after):
    slab = NG // pen
    width = width_of(slab)
    skip = first // ROWS
    near = jax.ShapeDtypeStruct((slab, width), jnp.bfloat16)
    far = jax.ShapeDtypeStruct((count, width), jnp.bfloat16)
    operands = [meta, orbitals, orbitals, depth_tables, cols_table]
    aliases = {len(operands) + s: s for s in range(len(earlier))}
    operands += [*earlier, *after]
    return pl.pallas_call(
        functools.partial(forward_kernel, slab, pen),
        out_shape=[near] * NEAR + [far] * (pen - NEAR),
        grid_spec=pltpu.PrefetchScalarGridSpec(
            num_scalar_prefetch=1,
            grid=(count // ROWS,),
            in_specs=[
                pl.BlockSpec((1, ROWS, NG * NG), lambda b, meta: (meta[0], b + skip, 0)),
                pl.BlockSpec((1, ROWS, NG * NG), lambda b, meta: (meta[1], b + skip, 0)),
                whole_spec(depth_tables.shape),
                whole_spec(cols_table.shape),
            ]
            + [pl.BlockSpec(memory_space=pl.ANY)] * (len(earlier) + len(after)),
            out_specs=[pl.BlockSpec((ROWS, width), lambda b, meta: (b + skip, 0))] * NEAR
            + [pl.BlockSpec((ROWS, width), lambda b, meta: (b, 0))] * (pen - NEAR),
            scratch_shapes=column_scratch() + [pltpu.VMEM((NG + NG // 2, LANE), jnp.float32)],
        ),
        input_output_aliases=aliases,
        compiler_params=pltpu.CompilerParams(vmem_limit_bytes=VMEM_BYTES),
        cost_estimate=pl.CostEstimate(
            flops=2 * 6 * count * NG * NG * NG, bytes_accessed=6 * count * NG * NG, transcendentals=0
        ),
        name="forward_planes",
    )(*operands)


def middle_columns(meta, fields, in_pieces, table, grid_table, part, pen, out_pieces, extra):
    slab = NG // pen
    width = width_of(slab)
    block = width // 8
    out_shapes, out_specs = [], []
    for s, first, count in out_pieces:
        if extra and first + count == slab:
            out_shapes.append(jax.ShapeDtypeStruct((count, width + LANE), jnp.bfloat16))
            out_specs.append(whole_spec((count, width + LANE)))
        else:
            out_shapes.append(jax.ShapeDtypeStruct((count, width), jnp.bfloat16))
            out_specs.append(pl.BlockSpec((count, block), lambda b, meta: (0, b)))
    in_specs = [whole_spec(table.shape), pl.BlockSpec((NG, block), lambda b, meta: (0, b)), whole_spec(part.shape)]
    in_specs += [pl.BlockSpec((count, block), lambda b, meta: (0, b)) for s, first, count in in_pieces]
    return pl.pallas_call(
        functools.partial(middle_kernel, pen, in_pieces, out_pieces, extra),
        out_shape=out_shapes,
        grid_spec=pltpu.PrefetchScalarGridSpec(
            num_scalar_prefetch=1,
            grid=(width // block,),
            in_specs=in_specs,
            out_specs=out_specs,
            scratch_shapes=[pltpu.VMEM((NG, block), jnp.bfloat16)],
        ),
        compiler_params=pltpu.CompilerParams(vmem_limit_bytes=VMEM_BYTES),
        cost_estimate=pl.CostEstimate(flops=2 * 5 * NG * NG * width, bytes_accessed=8 * NG * width, transcendentals=0),
        name="middle_columns",
    )(meta, table, grid_table, part, *fields)


def inverse_planes(meta, fields, orbitals, cols_table, depth_tables, pair, pairs, first, earlier, part_rows):
    pen = len(fields)
    slab = NG // pen
    count = fields[-1].shape[0]
    skip = first // ROWS
    out_shapes = [jax.ShapeDtypeStruct((pairs, slab, NG * NG), jnp.float32)]
    out_specs = [pl.BlockSpec((1, ROWS, NG * NG), lambda b, meta: (pair, b + skip, 0))]
    if part_rows:
        out_shapes.append(jax.ShapeDtypeStruct((part_rows, LANE), jnp.float32))
        out_specs.append(whole_spec((part_rows, LANE)))
    in_specs = [pl.BlockSpec((ROWS, field.shape[1]), lambda b, meta: (b + skip, 0)) for field in fields[:NEAR]]
    in_specs += [pl.BlockSpec((ROWS, field.shape[1]), lambda b, meta: (b, 0)) for field in fields[NEAR:]]
    in_specs += [
        pl.BlockSpec((1, ROWS, NG * NG), lambda b, meta: (meta[1], b + skip, 0)),
        whole_spec(cols_table.shape),
        whole_spec(depth_tables.shape),
    ]
    operands = [meta, *fields, orbitals, cols_table, depth_tables]
    aliases = {}
    if earlier is not None:
        aliases = {len(operands): 0}
        in_specs.append(pl.BlockSpec(memory_space=pl.ANY))
        operands.append(earlier)
    return pl.pallas_call(
        functools.partial(inverse_kernel, slab, pen, bool(part_rows)),
        out_shape=out_shapes,
        grid_spec=pltpu.PrefetchScalarGridSpec(
            num_scalar_prefetch=1,
            grid=(count // ROWS,),
            in_specs=in_specs,
            out_specs=out_specs,
            scratch_shapes=column_scratch(),
        ),
        input_output_aliases=aliases,
        compiler_params=pltpu.CompilerParams(vmem_limit_bytes=VMEM_BYTES),
        cost_estimate=pl.CostEstimate(
            flops=2 * 5 * count * NG * NG * NG, bytes_accessed=8 * count * NG * NG, transcendentals=0
        ),
        name="inverse_planes",
    )(*operands)


def exchange(s, field, pen):
    return lax.ppermute(field, "pen", [(i, i ^ s) for i in range(pen)]) if s else field


def stack_split(table):
    return np.concatenate(split_table(table), axis=0)


def depth_table_set():
    lanes = np.arange(2 * LANE)
    freq = np.where(lanes < NG, lanes, lanes - TAIL)
    tables = []
    for parity in range(2):
        depth = lanes - parity * TAIL
        inside = (depth >= 0) & (depth < NG)
        tables.append(np.where(inside[:, None], cas_table(depth[:, None], freq[None, :]), 0.0))
    return np.stack(split_table(np.stack(tables)), axis=1)


def grid_weights(me, slab):
    lane = jnp.arange(LANE, dtype=jnp.int32)[None, :]
    row = jnp.arange(slab, dtype=jnp.int32)[:, None]
    head_col, head_depth = jnp.broadcast_arrays(row, lane)
    tail_row = row[: slab // 2]
    tail_col = jnp.where(lane < TAIL, tail_row, tail_row + slab // 2)
    tail_depth = jnp.broadcast_to(LANE + lane % TAIL, tail_col.shape)
    col = signed_freq(me * slab + jnp.concatenate([head_col, tail_col], axis=0).reshape(-1), NG)
    depth = signed_freq(jnp.concatenate([head_depth, tail_depth], axis=0).reshape(-1), NG)
    plane = signed_freq(jnp.arange(NG, dtype=jnp.int32), NG)
    square_sum = (plane * plane)[:, None] + (col * col + depth * depth)[None, :]
    return coulomb_kernel(square_sum, NG) / float(NG * NG * NG)


def plane_runs(slab, first, last):
    if slab > ROWS and first:
        return ((0, ROWS), (ROWS, slab - ROWS))
    if slab > ROWS and last:
        return ((0, slab - ROWS), (slab - ROWS, ROWS))
    return ((0, slab),)


def pieces_of(pen, runs):
    far = tuple((s, first, count) for first, count in runs for s in range(pen - 1, NEAR - 1, -1))
    return far + tuple((s, 0, NG // pen) for s in range(NEAR - 1, -1, -1))


def both_parts(orbitals, pair_index, pen, coulomb_part):
    slab = NG // pen
    pairs = pair_index.shape[0]
    me = lax.axis_index("pen").astype(jnp.int32)
    positions = np.arange(NG)
    interleaved = np.concatenate([positions[0::2], positions[1::2]])
    depth_np = depth_table_set()
    depth_tables, depth_back = jnp.asarray(depth_np), jnp.asarray(np.swapaxes(depth_np, 2, 3))
    cols_forward = jnp.asarray(stack_split(cas_table(positions[:, None], interleaved[None, :])))
    cols_back = jnp.asarray(stack_split(cas_table(interleaved[:, None], positions[None, :])))
    plane_table = jnp.asarray(stack_split(cas_table(positions[:, None], positions[None, :])))
    metas = [jnp.concatenate([pair_index[p], me[None]]) for p in range(pairs)]

    held, after = [], []
    for p in range(pairs):
        runs = plane_runs(slab, p == 0, False)
        taken, made = {}, ()
        for first, count in runs:
            made = forward_planes(
                metas[p], orbitals, depth_tables, cols_forward, pen, first, count, made[:NEAR], after if first == 0 else ()
            )
            for s in range(NEAR, pen):
                taken[s, first] = exchange(s, made[s], pen)
        for s in range(NEAR):
            taken[s, 0] = exchange(s, made[s], pen)
        pieces = pieces_of(pen, runs)
        held.append((pieces, [taken[s, first] for s, first, count in pieces]))
        if p == 0:
            local, part_of = coulomb_part(made[-1])
            after = [local] + [taken[s, 0] for s in range(NEAR, pen) if len(runs) > 1]
    late_me, _ = lax.optimization_barrier((me, made[-1]))
    grid_table = grid_weights(late_me, slab)
    part = part_of(local)

    back = []
    for p in range(pairs):
        last = p == pairs - 1
        fed = part if last else jnp.zeros_like(part)
        runs = plane_runs(slab, False, last)
        pieces = pieces_of(pen, runs)
        filtered = middle_columns(metas[p], held[p][1], held[p][0], plane_table, grid_table, fed, pen, pieces, last)
        back.append((runs, {piece[:2]: exchange(piece[0], field, pen) for piece, field in zip(pieces, filtered)}))

    terms = None
    for p in range(pairs):
        runs, taken = back[p]
        for first, count in runs:
            final = p == pairs - 1 and first + count == slab
            fields = [taken[s, 0 if s < NEAR else first] for s in range(pen)]
            made = inverse_planes(
                metas[p], fields, orbitals, cols_back, depth_back, p, pairs, first, terms, part.shape[1] if final else 0
            )
            terms = made[0]
    return made[1], terms


def pair_fields_plain(orbitals, pair_index, pen):
    slab = NG // pen
    plane_rows = orbitals.shape[1]
    positions = jnp.arange(NG, dtype=jnp.int32)
    places = np.arange(NG)
    high, low = (jnp.asarray(part) for part in split_table(cas_table(places[:, None], places[None, :])))

    def transform(axes, field):
        first = lax.reduce_precision(field, 8, 7)
        second = (field - first).astype(jnp.bfloat16)
        first = first.astype(jnp.bfloat16)
        return (
            jnp.einsum(axes, first, high, preferred_element_type=jnp.float32)
            + jnp.einsum(axes, first, low, preferred_element_type=jnp.float32)
            + jnp.einsum(axes, second, high, preferred_element_type=jnp.float32)
        )

    grid = orbitals.reshape(orbitals.shape[0], plane_rows, NG, NG)
    right = grid[pair_index[:, 1]].astype(jnp.float32)
    field = grid[pair_index[:, 0]].astype(jnp.float32) * right
    field = transform("pxyk,yv->pxvk", transform("pxyz,zk->pxyk", field))
    field = lax.all_to_all(field.astype(jnp.bfloat16), "pen", split_axis=2, concat_axis=1, tiled=True)
    col = signed_freq(lax.axis_index("pen") * slab + jnp.arange(slab, dtype=jnp.int32), NG)
    freq = signed_freq(positions, NG)
    square_sum = (freq * freq)[:, None, None] + (col * col)[None, :, None] + (freq * freq)[None, None, :]
    weights = coulomb_kernel(square_sum, NG) / float(NG * NG * NG)
    field = transform("pxyk,xv->pvyk", field.astype(jnp.float32)) * weights[None]
    field = transform("pxyk,xv->pvyk", field).astype(jnp.bfloat16)
    field = lax.all_to_all(field, "pen", split_axis=1, concat_axis=2, tiled=True)
    field = transform("pxyk,yv->pxvk", field.astype(jnp.float32))
    terms = transform("pxyk,kz->pxyz", field) * right
    return terms.reshape(terms.shape[0], plane_rows, NG * NG)


def tile_pass(tile_blocks, aux_local, pair_ids, live_count, contribute, initial):
    step_rows = 8

    def add_block(step_index, running):
        first_slot = step_index * step_rows
        tile_block = lax.dynamic_slice_in_dim(tile_blocks, first_slot, step_rows, 0)
        aux_block = lax.dynamic_slice_in_dim(aux_local, first_slot, step_rows, 0)
        pair_block = lax.dynamic_slice_in_dim(pair_ids, first_slot, step_rows, 0)
        slot_ids = first_slot + jnp.arange(step_rows, dtype=jnp.int32)
        live_mask = (slot_ids < live_count).astype(jnp.float32)
        return contribute(running, tile_block, aux_block, pair_block, live_mask)

    block_count = (live_count + step_rows - 1) // step_rows
    return lax.fori_loop(0, block_count, add_block, initial)


def coulomb_partial(tile_blocks, tile_aux, tile_pair, tile_count, density, metric_inv):
    aux_count = metric_inv.shape[0]
    dens_all = lax.all_gather(density, "blk", axis=0, tiled=True)
    aux_local = tile_aux - lax.axis_index("pen") * aux_count
    live_count = tile_count[0]
    aux_ids = jnp.arange(aux_count, dtype=jnp.int32)

    def add_fit(running, tile_block, aux_block, pair_block, live_mask):
        dens_rows = dens_all[pair_block]
        partial_value = jnp.einsum("tap,tp->ta", tile_block, dens_rows, preferred_element_type=jnp.float32)
        partial_value = partial_value * live_mask[:, None]
        selector = (aux_block[:, None] == aux_ids[None, :]).astype(jnp.float32)
        return running + jnp.einsum("tk,ta->ka", selector, partial_value, precision=PRECISE)

    gamma = jnp.zeros((aux_count, tile_blocks.shape[1]), jnp.float32)
    gamma = tile_pass(tile_blocks, aux_local, tile_pair, live_count, add_fit, gamma)
    gamma_all = lax.psum(gamma, ("grp", "blk"))
    coef = jnp.einsum("kab,kb->ka", metric_inv, gamma_all, precision=PRECISE).astype(jnp.bfloat16)

    def add_coulomb(running, tile_block, aux_block, pair_block, live_mask):
        selector = (aux_block[:, None] == aux_ids[None, :]).astype(jnp.bfloat16)
        coef_rows = jnp.dot(selector, coef, preferred_element_type=jnp.float32).astype(jnp.bfloat16)
        partial_value = jnp.einsum("tap,ta->tp", tile_block, coef_rows, preferred_element_type=jnp.float32)
        partial_value = partial_value * live_mask[:, None]
        return running.at[pair_block].add(partial_value)

    part = jnp.zeros((dens_all.shape[0], tile_blocks.shape[2]), jnp.float32)
    return tile_pass(tile_blocks, aux_local, tile_pair, live_count, add_coulomb, part)


def body(tile_blocks, tile_aux, tile_pair, tile_count, density, metric_inv, orbitals, pair_index):
    pen, blk, grp = (lax.axis_size(name) for name in ("pen", "blk", "grp"))
    slab = orbitals.shape[1]
    rows = density.shape[0] // (grp * pen)
    tiles = (tile_blocks, tile_aux, tile_pair, tile_count)
    if slab % ROWS == 0 and pen & (pen - 1) == 0 and pen >= NEAR and rows <= ROWS // 3:

        def coulomb_part(after):
            late_density, _ = lax.optimization_barrier((density, after))
            return coulomb_partial(*tiles, late_density, metric_inv), sum_part

        def sum_part(local):
            shares = local.reshape(grp, pen, blk, rows, LANE).transpose(0, 2, 1, 3, 4)
            shares = shares.reshape(grp * blk, pen * rows, LANE)
            taken = lax.all_to_all(shares, ("grp", "blk"), split_axis=0, concat_axis=0, tiled=True)
            return taken.sum(axis=0).reshape(pen, rows, LANE)

        return both_parts(orbitals, pair_index, pen, coulomb_part)
    part = coulomb_partial(*tiles, density, metric_inv)
    coulomb = lax.psum_scatter(part, ("grp", "pen", "blk"), scatter_dimension=0, tiled=True)
    return coulomb, pair_fields_plain(orbitals, pair_index, pen)


def solution(mesh):
    placed = (
        P(("grp", "pen", "blk"), None, None),
        P(("grp", "pen", "blk")),
        P(("grp", "pen", "blk")),
        P(("grp", "pen", "blk")),
        P("blk", None),
        P("pen", None, None),
        P(None, "pen", None),
        P(("grp", "blk"), None),
    )
    return jax.shard_map(
        body,
        mesh=mesh,
        in_specs=placed,
        out_specs=(P(("grp", "pen", "blk"), None), P(("grp", "blk"), "pen", None)),
        check_vma=False,
    )
```

time: 2150 us -> 330 us (0.15)
  waiting for transfers between devices: 1220 us -> 120 us
  matrix products: 357 us -> 2.63 us
  local copies, waits for them, and re-layouts: 245 us -> 7.18 us
  other arithmetic: 256 us -> 34.2 us
  Pallas kernels: 0 us -> 102 us
    unnamed x2 -> x0, waiting for transfers between devices: 662 us -> none
    all_to_all x2 -> x0, waiting for transfers between devices: 563 us -> none  [the longest x1 563 us: body(): lax.all_to_all(freq_data, 'pen', split_axis=2, concat_axis=1, tiled=True)]
    dot_general x11 -> x1, matrix products: 354 us -> 0.92 us  [coulomb_partial(): jnp.einsum('kab,kb->ka', metric_inv, gamma_all, precision=PRECISE)]
    ppermute x0 -> x16, waiting for transfers between devices: none -> 120 us  [exchange(): lax.ppermute(field, 'pen', [(i, i ^ s) for i in range(pen)])]
    pallas_call x0 -> x8, Pallas kernels: none -> 102 us  [the longest x3 40.3 us: forward_planes(): pl.pallas_call(functools.partial(forward_kernel, slab, pen), out_shape=[n...]
    sub x3 -> x1, other arithmetic: 75.8 us -> 0.01 us  [coulomb_partial(): aux_local = tile_aux - lax.axis_index('pen') * aux_count]
    add x3 -> x2, other arithmetic: 75.6 us -> 0.03 us  [the longest x1 0.02 us: grid_weights(): square_sum = (plane * plane)[:, None] + (col * col + depth * depth)[None, :]]
    reshape x2 -> x1, local copies, waits for them, and re-layouts: 75.2 us -> 0.01 us  [sum_part(): shares = local.reshape(grp, pen, blk, rows, LANE).transpose(0, 2, 1, 3, 4)]
  transfers between devices with their start and end apart: 3 -> 16, of which waited for: 2 -> 5; matrix products, arithmetic and copies ran while one was open for 3% -> 12% of each run, Pallas kernels for 0% -> 26%
where the time goes in v1:
time: 330 us; the launch traced here: 329 us
  waiting for transfers between devices  120 us (36%)
  Pallas kernels  102 us (31%)
  other arithmetic  34.2 us (10%)
  blocking collectives  32.7 us (10%)
  starting transfers between devices  29.6 us (9%)
  local copies, waits for them, and re-layouts  7.18 us (2%)
    ppermute x16, waiting for transfers between devices, exchange(): lax.ppermute(field, 'pen', [(i, i ^ s) for i in range(pen)])  120 us
    pallas_call x3, Pallas kernels, forward_planes(): pl.pallas_call(functools.partial(forward_kernel, slab, pen), out_shape=[n...  40.3 us
    pallas_call x3, Pallas kernels, inverse_planes(): pl.pallas_call(functools.partial(inverse_kernel, slab, pen, bool(part_row...  36.6 us
    ppermute x16, starting transfers between devices, exchange(): lax.ppermute(field, 'pen', [(i, i ^ s) for i in range(pen)])  29.6 us
    div x1, other arithmetic, grid_weights(): return coulomb_kernel(square_sum, NG) / float(NG * NG * NG)  27.8 us
    pallas_call x2, Pallas kernels, middle_columns(): pl.pallas_call(functools.partial(middle_kernel, pen, in_pieces, out_piece...  24.8 us
    psum x1, blocking collectives, coulomb_partial(): gamma_all = lax.psum(gamma, ('grp', 'blk'))  17.2 us
    all_gather x1, blocking collectives, coulomb_partial(): dens_all = lax.all_gather(density, 'blk', axis=0, tiled=True)  8.19 us
  transfers between devices with their start and end apart: 16, of which 5 were waited for; matrix products, arithmetic and copies ran while one was open for 12% of the time, Pallas kernels for 26%

profile of v1, /device:TPU:8, one launch (start us, length us, event | category | flops | bytes accessed | tf_op | source)
XLA Modules:
  0.0 329.2 jit_solution(2939743769063821428)
XLA Ops:
  2.0 8.4 %forward_planes.3 = (bf16[48,9216]{1,0:T(8,128)(2,1)}, bf16[48,9216]{1,0:T(8,128)(2,1)}, bf16[16,9216]{1,0:T(8,128)(2,1)}, bf16[16,9216]{1,0:T(8,128)(2,1)}) custom-call(s32[3]{0:T(128)} %pad_add_fusion.1.meta_ref, bf16[8,48,36864]{2,1,0:T(8,128)(2,1)} %refs_4_.5, bf16[8,48,36864]{2,1,0:T(8,128)(2,1)} %refs_4_.5, ...), custom_call_target="tpu_custom_call" | custom-call | flops 1358954496 | bytes 3538944 | tf_op jit(solution)/shard_map/forward_planes/pallas_call | solution.py:251
  13.0 13.6 %forward_planes.4 = (bf16[48,9216]{1,0:T(8,128)(2,1)}, bf16[48,9216]{1,0:T(8,128)(2,1)}, bf16[32,9216]{1,0:T(8,128)(2,1)}, bf16[32,9216]{1,0:T(8,128)(2,1)}) custom-call(s32[3]{0:T(128)} %pad_add_fusion.1.meta_ref, bf16[8,48,36864]{2,1,0:T(8,128)(2,1)} %refs_4_.5, bf16[8,48,36864]{2,1,0:T(8,128)(2,1)} %refs_4_.5, ...), custom_call_target="tpu_custom_call", output_to_operand_aliasing={{0}: (5, {}), {1}: (6, {})} | custom-call | flops 2717908992 | bytes 7077888 | tf_op jit(solution)/shard_map/forward_planes/pallas_call | solution.py:251
  26.6 2.8 collective-permute-start.11
  31.7 8.2 %all_gather.3 = bf16[128,128]{1,0:T(8,128)(2,1)S(1)} all-gather(bf16[32,128]{1,0:T(8,128)(2,1)S(1)} %copy-done.13), channel_id=1, replica_groups=mesh['grp'=2,'pen'=4,'blk'=4] {'blk'}, dimensions={0}, use_global_device_ids=true | all-gather | bytes 40960 | tf_op jit(solution)/shard_map/all_gather | solution.py:503
  40.0 3.8 %while.22 = (s32[]{:T(128)}, f32[8,128]{1,0:T(8,128)S(1)}, s32[]{:T(128)}, s32[32]{0:T(128)S(1)}, bf16[32,128,128]{2,1,0:T(8,128)(2,1)S(1)}, /*index=5*/s32[32]{...) while((s32[]{:T(128)}, f32[8,128]{1,0:T(8,128)S(1)}, ...), condition=%wide.region_1.2_spmd.clone, body=%wide.region_0.1_spmd.clone.sunk | while | flops 363638 | bytes 289239 | solution.py:498
  43.8 17.2 %psum.7 = f32[8,128]{1,0:T(8,128)S(1)} all-reduce(f32[8,128]{1,0:T(8,128)S(1)} %get-tuple-element.128), channel_id=1, replica_groups=mesh['grp'=2,'pen'=4,'blk'=4] {'grp','blk'}, use_global_device_ids=true, to_apply=%region_2.3 | all-reduce | flops 1024 | bytes 8192 | tf_op jit(solution)/shard_map/psum | solution.py:517
  61.9 3.9 %while.23 = (s32[]{:T(128)}, f32[128,128]{1,0:T(8,128)S(1)}, s32[]{:T(128)}, s32[32]{0:T(128)S(1)}, bf16[32,128,128]{2,1,0:T(8,128)(2,1)S(1)}, /*index=5*/s32[32...) while((s32[]{:T(128)}, f32[128,128]{1,0:T(8,128)S(1)}, ...), condition=%wide.region_5.6_spmd.clone, body=%wide.region_3.5_spmd.clone.sunk | while | flops 281718 | bytes 342903 | solution.py:498
  67.3 18.4 %forward_planes.5 = (bf16[48,9216]{1,0:T(8,128)(2,1)}, bf16[48,9216]{1,0:T(8,128)(2,1)}, bf16[48,9216]{1,0:T(8,128)(2,1)}, bf16[48,9216]{1,0:T(8,128)(2,1)}) custom-call(s32[3]{0:T(128)} %pad_add_fusion.meta_ref, bf16[8,48,36864]{2,1,0:T(8,128)(2,1)} %refs_4_.5, bf16[8,48,36864]{2,1,0:T(8,128)(2,1)} %refs_4_.5, ...), custom_call_target="tpu_custom_call" | custom-call | flops 4076863488 | bytes 10616832 | tf_op jit(solution)/shard_map/forward_planes/pallas_call | solution.py:251
  85.6 6.8 %collective-permute-start.2 = (bf16[48,9216]{1,0:T(8,128)(2,1)}, bf16[48,9216]{1,0:T(8,128)(2,1)}, u32[]{:S(2)}, u32[]{:S(2)}) collective-permute-start(bf16[48,9216]{1,0:T(8,128)(2,1)} %get-tuple-element.132), channel_id=1, source_target_pairs={{0,12},{4,8},{8,4},{12,0},{1,13},{5,9},{9,5},{13,1},{2,14},{6,10},... | collective-permute-start | bytes 2654216 | tf_op jit(solution)/shard_map/ppermute | solution.py:350
  94.1 27.8 %fusion.23.grid_ref = f32[192,9216]{1,0:T(8,128)} fusion(s32[9216]{0:T(1024)S(1)} %fusion.30, s32[192]{0:T(256)S(1)} %fusion.33), kind=kLoop, calls=%fused_computation.34 | loop fusion | flops 17694720 | bytes 7115520 | tf_op jit(solution)/shard_map/div | solution.py:379
  121.9 5.0 %collective-permute-done.10.refs_2_ = bf16[32,9216]{1,0:T(8,128)(2,1)} collective-permute-done((bf16[32,9216]{1,0:T(8,128)(2,1)}, bf16[32,9216]{1,0:T(8,128)(2,1)}, u32[]{:S(2)}, u32[]{:S(2)}) %collective-permute-start.10) | collective-permute-done | bytes 589856 | tf_op jit(solution)/shard_map/ppermute | solution.py:350
  127.9 12.2 %middle_columns.3 = (bf16[48,9216]{1,0:T(8,128)(2,1)}, bf16[48,9216]{1,0:T(8,128)(2,1)}, bf16[48,9216]{1,0:T(8,128)(2,1)}, bf16[48,9216]{1,0:T(8,128)(2,1)}) custom-call(s32[3]{0:T(128)} %pad_add_fusion.1.meta_ref, bf16[384,192]{1,0:T(8,128)(2,1)} %constant.113.clone.table_ref, f32[192,9216]{1,0:T(8,128)} %fusion.23.grid_ref, ...), custom_call_target="tpu_custom_call" | custom-call | flops 3397386240 | bytes 14155776 | tf_op jit(solution)/shard_map/middle_columns/pallas_call | solution.py:291
  140.2 7.3 %all_to_all.5 = f32[8,16,128]{2,1,0:T(8,128)S(1)} all-to-all(f32[8,16,128]{2,1,0:T(8,128)S(1)} %bitcast.52), channel_id=1, replica_groups=mesh['grp'=2,'pen'=4,'blk'=4] {'grp','blk'}, dimensions={0} | all-to-all | bytes 131072 | tf_op jit(solution)/shard_map/all_to_all | solution.py:545
  148.1 4.0 %collective-permute-start.14 = (bf16[48,9216]{1,0:T(8,128)(2,1)}, bf16[48,9216]{1,0:T(8,128)(2,1)S(1)}, u32[]{:S(2)}, u32[]{:S(2)}) collective-permute-start(bf16[48,9216]{1,0:T(8,128)(2,1)} %get-tuple-element.148), channel_id=1, source_target_pairs={{0,8},{4,12},{8,0},{12,4},{1,9},{5,13},{9,1},{13,5},{2,10},{6,14},... | collective-permute-start | bytes 2654216 | tf_op jit(solution)/shard_map/ppermute | solution.py:350
  152.2 31.8 %collective-permute-done.3.refs_1_ = bf16[48,9216]{1,0:T(8,128)(2,1)} collective-permute-done((bf16[48,9216]{1,0:T(8,128)(2,1)}, bf16[48,9216]{1,0:T(8,128)(2,1)}, u32[]{:S(2)}, u32[]{:S(2)}) %collective-permute-start.3) | collective-permute-done | bytes 884768 | tf_op jit(solution)/shard_map/ppermute | solution.py:350
  184.0 12.6 %middle_columns.2 = (bf16[32,9216]{1,0:T(8,128)(2,1)}, bf16[32,9216]{1,0:T(8,128)(2,1)}, bf16[16,9344]{1,0:T(8,128)(2,1)}, bf16[16,9344]{1,0:T(8,128)(2,1)}, bf1...) custom-call(s32[3]{0:T(128)} %pad_add_fusion.meta_ref, bf16[384,192]{1,0:T(8,128)(2,1)} %constant.113.clone.table_ref, ...), custom_call_target="tpu_custom_call" | custom-call | flops 3397386240 | bytes 14155776 | tf_op jit(solution)/shard_map/middle_columns/pallas_call | solution.py:291
  196.6 4.9 %collective-permute-start.5 = (bf16[48,9344]{1,0:T(8,128)(2,1)}, bf16[48,9344]{1,0:T(8,128)(2,1)S(1)}, u32[]{:S(2)}, u32[]{:S(2)}) collective-permute-start(bf16[48,9344]{1,0:T(8,128)(2,1)} %get-tuple-element.138), channel_id=1, source_target_pairs={{0,4},{4,0},{8,12},{12,8},{1,5},{5,1},{9,13},{13,9},{2,6},{6,2},{1... | collective-permute-start | bytes 2691080 | tf_op jit(solution)/shard_map/ppermute | solution.py:350
  203.1 18.9 %collective-permute-done.14.refs_2_ = bf16[48,9216]{1,0:T(8,128)(2,1)S(1)} collective-permute-done((bf16[48,9216]{1,0:T(8,128)(2,1)}, bf16[48,9216]{1,0:T(8,128)(2,1)S(1)}, u32[]{:S(2)}, u32[]{:S(2)}) %collective-permute-start.14) | collective-permute-done | bytes 884768 | tf_op jit(solution)/shard_map/ppermute | solution.py:350
  222.0 3.3 collective-permute-start.6
  225.3 55.8 %collective-permute-done.15.refs_3_ = bf16[48,9216]{1,0:T(8,128)(2,1)S(1)} collective-permute-done((bf16[48,9216]{1,0:T(8,128)(2,1)}, bf16[48,9216]{1,0:T(8,128)(2,1)S(1)}, u32[]{:S(2)}, u32[]{:S(2)}) %collective-permute-start.15) | collective-permute-done | bytes 884768 | tf_op jit(solution)/shard_map/ppermute | solution.py:350
  282.0 16.3 %inverse_planes.3.refs_7_ = f32[2,48,36864]{2,1,0:T(8,128)} custom-call(s32[3]{0:T(128)} %pad_add_fusion.1.meta_ref, bf16[48,9216]{1,0:T(8,128)(2,1)} %get-tuple-element.146.refs_0_, bf16[48,9216]{1,0:T(8,128)(2,1)} %copy-done.4, bf16[48,9216]{1,0:T(8,128)(2,1)} %copy-done.5, bf16[48,9216]{1,0:T(8,128)(2,1)} %copy-done.6, bf16[8,48,36864]{2,1,0:T(8,128)(2,1)} %refs_4_.5, ...), custom_call_target="tpu_custom_call" | custom-call | flops 3397386240 | bytes 14155776 | tf_op jit(solution)/shard_map/inverse_planes/pallas_call | solution.py:330
  298.3 8.1 %collective-permute-done.9.refs_3_ = bf16[32,9216]{1,0:T(8,128)(2,1)S(1)} collective-permute-done((bf16[32,9216]{1,0:T(8,128)(2,1)}, bf16[32,9216]{1,0:T(8,128)(2,1)S(1)}, u32[]{:S(2)}, u32[]{:S(2)}) %collective-permute-start.9) | collective-permute-done | bytes 589856 | tf_op jit(solution)/shard_map/ppermute | solution.py:350
  307.5 12.2 %inverse_planes.4.refs_7_ = f32[2,48,36864]{2,1,0:T(8,128)} custom-call(s32[3]{0:T(128)} %pad_add_fusion.meta_ref, bf16[48,9344]{1,0:T(8,128)(2,1)} %get-tuple-element.137.refs_0_, bf16[48,9344]{1,0:T(8,128)(2,1)} %copy-done.3, bf16[32,9216]{1,0:T(8,128)(2,1)} %copy-done.7, bf16[32,9216]{1,0:T(8,128)(2,1)} %copy-done.8, ...), custom_call_target="tpu_custom_call", output_to_operand_aliasing={{}: (8, {})} | custom-call | flops 2264924160 | bytes 9437184 | tf_op jit(solution)/shard_map/inverse_planes/pallas_call | solution.py:330
  321.1 8.1 %inverse_planes.5 = (f32[2,48,36864]{2,1,0:T(8,128)}, f32[4,128]{1,0:T(4,128)}) custom-call(s32[3]{0:T(128)} %pad_add_fusion.meta_ref, bf16[48,9344]{1,0:T(8,128)(2,1)} %get-tuple-element.137.refs_0_, bf16[48,9344]{1,0:T(8,128)(2,1)} %copy-done.3, bf16[16,9344]{1,0:T(8,128)(2,1)} %copy-done.9, ...), custom_call_target="tpu_custom_call", output_to_operand_aliasing={{0}: (8, {})} | custom-call | flops 1132462080 | bytes 4718592 | tf_op jit(solution)/shard_map/inverse_planes/pallas_call | solution.py:330
  (103 shorter events, 23.8 us)
Async XLA Ops:
  0.6 60.3 %copy-start = (f32[8,128,128]{2,1,0:T(8,128)S(1)}, f32[8,128,128]{2,1,0:T(8,128)}, u32[]{:S(2)}) copy-start(f32[8,128,128]{2,1,0:T(8,128)} %param.22) | copy-start | bytes 1572868
  10.4 56.0 %collective-permute-start = (bf16[16,9216]{1,0:T(8,128)(2,1)}, bf16[16,9216]{1,0:T(8,128)(2,1)S(1)}, u32[]{:S(2)}, u32[]{:S(2)}) collective-permute-start(bf16[16,9216]{1,0:T(8,128)(2,1)} %get-tuple-element.130), channel_id=1, source_target_pairs={{0,8},{4,12},{8,0},{12,4},{1,9},{5,13},{9,1},{13,5},{2,10},{6,14},... | collective-permute-start | bytes 884744 | tf_op jit(solution)/shard_map/ppermute | solution.py:350
  13.0 53.4 %collective-permute-start.1 = (bf16[16,9216]{1,0:T(8,128)(2,1)}, bf16[16,9216]{1,0:T(8,128)(2,1)S(1)}, u32[]{:S(2)}, u32[]{:S(2)}) collective-permute-start(bf16[16,9216]{1,0:T(8,128)(2,1)} %get-tuple-element.131), channel_id=1, source_target_pairs={{0,12},{4,8},{8,4},{12,0},{1,13},{5,9},{9,5},{13,1},{2,14},{6,10},... | collective-permute-start | bytes 884744 | tf_op jit(solution)/shard_map/ppermute | solution.py:350
  13.0 18.7 %copy-start.13 = (bf16[32,128]{1,0:T(8,128)(2,1)S(1)}, bf16[32,128]{1,0:T(8,128)(2,1)}, u32[]{:S(2)}) copy-start(bf16[32,128]{1,0:T(8,128)(2,1)} %param.21) | copy-start | bytes 24580
  13.0 26.9 %copy-start.15 = (s32[32]{0:T(128)S(1)}, s32[32]{0:T(128)}, u32[]{:S(2)}) copy-start(s32[32]{0:T(128)} %param.18) | copy-start | bytes 388
  13.0 26.9 %copy-start.2 = (bf16[32,128,128]{2,1,0:T(8,128)(2,1)S(1)}, bf16[32,128,128]{2,1,0:T(8,128)(2,1)}, u32[]{:S(2)}) copy-start(bf16[32,128,128]{2,1,0:T(8,128)(2,1)} %param.17) | copy-start | bytes 3145732
  13.0 26.9 %copy-start.16 = (s32[32]{0:T(128)S(1)}, s32[32]{0:T(128)}, u32[]{:S(2)}) copy-start(s32[32]{0:T(128)} %param.19) | copy-start | bytes 388
  26.6 65.9 %collective-permute-start.11 = (bf16[32,9216]{1,0:T(8,128)(2,1)}, bf16[32,9216]{1,0:T(8,128)(2,1)}, u32[]{:S(2)}, u32[]{:S(2)}) collective-permute-start(bf16[32,9216]{1,0:T(8,128)(2,1)} %get-tuple-element.143), channel_id=1, source_target_pairs={{0,8},{4,12},{8,0},{12,4},{1,9},{5,13},{9,1},{13,5},{2,10},{6,14},... | collective-permute-start | bytes 1769480 | tf_op jit(solution)/shard_map/ppermute | solution.py:350
  29.4 97.5 %collective-permute-start.10 = (bf16[32,9216]{1,0:T(8,128)(2,1)}, bf16[32,9216]{1,0:T(8,128)(2,1)}, u32[]{:S(2)}, u32[]{:S(2)}) collective-permute-start(bf16[32,9216]{1,0:T(8,128)(2,1)} %get-tuple-element.126), channel_id=1, source_target_pairs={{0,12},{4,8},{8,4},{12,0},{1,13},{5,9},{9,5},{13,1},{2,14},{6,10},... | collective-permute-start | bytes 1769480 | tf_op jit(solution)/shard_map/ppermute | solution.py:350
  29.9 97.1 %collective-permute-start.12 = (bf16[48,9216]{1,0:T(8,128)(2,1)}, bf16[48,9216]{1,0:T(8,128)(2,1)S(1)}, u32[]{:S(2)}, u32[]{:S(2)}) collective-permute-start(bf16[48,9216]{1,0:T(8,128)(2,1)} %get-tuple-element.144), channel_id=1, source_target_pairs={{0,4},{4,0},{8,12},{12,8},{1,5},{5,1},{9,13},{13,9},{2,6},{6,2},{1... | collective-permute-start | bytes 2654216 | tf_op jit(solution)/shard_map/ppermute | solution.py:350
  85.6 98.3 %collective-permute-start.2 = (bf16[48,9216]{1,0:T(8,128)(2,1)}, bf16[48,9216]{1,0:T(8,128)(2,1)}, u32[]{:S(2)}, u32[]{:S(2)}) collective-permute-start(bf16[48,9216]{1,0:T(8,128)(2,1)} %get-tuple-element.132), channel_id=1, source_target_pairs={{0,12},{4,8},{8,4},{12,0},{1,13},{5,9},{9,5},{13,1},{2,14},{6,10},... | collective-permute-start | bytes 2654216 | tf_op jit(solution)/shard_map/ppermute | solution.py:350
  92.4 91.5 %collective-permute-start.3 = (bf16[48,9216]{1,0:T(8,128)(2,1)}, bf16[48,9216]{1,0:T(8,128)(2,1)}, u32[]{:S(2)}, u32[]{:S(2)}) collective-permute-start(bf16[48,9216]{1,0:T(8,128)(2,1)} %get-tuple-element.134), channel_id=1, source_target_pairs={{0,8},{4,12},{8,0},{12,4},{1,9},{5,13},{9,1},{13,5},{2,10},{6,14},... | collective-permute-start | bytes 2654216 | tf_op jit(solution)/shard_map/ppermute | solution.py:350
  92.5 91.5 %collective-permute-start.4 = (bf16[48,9216]{1,0:T(8,128)(2,1)}, bf16[48,9216]{1,0:T(8,128)(2,1)}, u32[]{:S(2)}, u32[]{:S(2)}) collective-permute-start(bf16[48,9216]{1,0:T(8,128)(2,1)} %get-tuple-element.135), channel_id=1, source_target_pairs={{0,4},{4,0},{8,12},{12,8},{1,5},{5,1},{9,13},{13,9},{2,6},{6,2},{1... | collective-permute-start | bytes 2654216 | tf_op jit(solution)/shard_map/ppermute | solution.py:350
  140.1 61.4 %collective-permute-start.13 = (bf16[48,9216]{1,0:T(8,128)(2,1)}, bf16[48,9216]{1,0:T(8,128)(2,1)S(1)}, u32[]{:S(2)}, u32[]{:S(2)}) collective-permute-start(bf16[48,9216]{1,0:T(8,128)(2,1)} %get-tuple-element.147), channel_id=1, source_target_pairs={{0,4},{4,0},{8,12},{12,8},{1,5},{5,1},{9,13},{13,9},{2,6},{6,2},{1... | collective-permute-start | bytes 2654216 | tf_op jit(solution)/shard_map/ppermute | solution.py:350
  148.1 73.9 %collective-permute-start.14 = (bf16[48,9216]{1,0:T(8,128)(2,1)}, bf16[48,9216]{1,0:T(8,128)(2,1)S(1)}, u32[]{:S(2)}, u32[]{:S(2)}) collective-permute-start(bf16[48,9216]{1,0:T(8,128)(2,1)} %get-tuple-element.148), channel_id=1, source_target_pairs={{0,8},{4,12},{8,0},{12,4},{1,9},{5,13},{9,1},{13,5},{2,10},{6,14},... | collective-permute-start | bytes 2654216 | tf_op jit(solution)/shard_map/ppermute | solution.py:350
  184.0 97.1 %collective-permute-start.15 = (bf16[48,9216]{1,0:T(8,128)(2,1)}, bf16[48,9216]{1,0:T(8,128)(2,1)S(1)}, u32[]{:S(2)}, u32[]{:S(2)}) collective-permute-start(bf16[48,9216]{1,0:T(8,128)(2,1)} %get-tuple-element.149), channel_id=1, source_target_pairs={{0,12},{4,8},{8,4},{12,0},{1,13},{5,9},{9,5},{13,1},{2,14},{6,10},... | collective-permute-start | bytes 2654216 | tf_op jit(solution)/shard_map/ppermute | solution.py:350
  196.6 109.8 %collective-permute-start.5 = (bf16[48,9344]{1,0:T(8,128)(2,1)}, bf16[48,9344]{1,0:T(8,128)(2,1)S(1)}, u32[]{:S(2)}, u32[]{:S(2)}) collective-permute-start(bf16[48,9344]{1,0:T(8,128)(2,1)} %get-tuple-element.138), channel_id=1, source_target_pairs={{0,4},{4,0},{8,12},{12,8},{1,5},{5,1},{9,13},{13,9},{2,6},{6,2},{1... | collective-permute-start | bytes 2691080 | tf_op jit(solution)/shard_map/ppermute | solution.py:350
  201.5 96.8 %collective-permute-start.8 = (bf16[32,9216]{1,0:T(8,128)(2,1)}, bf16[32,9216]{1,0:T(8,128)(2,1)S(1)}, u32[]{:S(2)}, u32[]{:S(2)}) collective-permute-start(bf16[32,9216]{1,0:T(8,128)(2,1)} %get-tuple-element.141), channel_id=1, source_target_pairs={{0,8},{4,12},{8,0},{12,4},{1,9},{5,13},{9,1},{13,5},{2,10},{6,14},... | collective-permute-start | bytes 1769480 | tf_op jit(solution)/shard_map/ppermute | solution.py:350
  201.5 79.9 %copy-start.4 = (bf16[48,9216]{1,0:T(8,128)(2,1)}, bf16[48,9216]{1,0:T(8,128)(2,1)S(1)}, u32[]{:S(2)}) copy-start(bf16[48,9216]{1,0:T(8,128)(2,1)S(1)} %collective-permute-done.13.refs_1_) | copy-start | bytes 2654212
  201.5 104.8 %collective-permute-start.9 = (bf16[32,9216]{1,0:T(8,128)(2,1)}, bf16[32,9216]{1,0:T(8,128)(2,1)S(1)}, u32[]{:S(2)}, u32[]{:S(2)}) collective-permute-start(bf16[32,9216]{1,0:T(8,128)(2,1)} %get-tuple-element.142), channel_id=1, source_target_pairs={{0,12},{4,8},{8,4},{12,0},{1,13},{5,9},{9,5},{13,1},{2,14},{6,10},... | collective-permute-start | bytes 1769480 | tf_op jit(solution)/shard_map/ppermute | solution.py:350
  222.0 59.4 %copy-start.5 = (bf16[48,9216]{1,0:T(8,128)(2,1)}, bf16[48,9216]{1,0:T(8,128)(2,1)S(1)}, u32[]{:S(2)}) copy-start(bf16[48,9216]{1,0:T(8,128)(2,1)S(1)} %collective-permute-done.14.refs_2_) | copy-start | bytes 2654212
  222.0 97.7 %collective-permute-start.6 = (bf16[16,9344]{1,0:T(8,128)(2,1)}, bf16[16,9344]{1,0:T(8,128)(2,1)S(1)}, u32[]{:S(2)}, u32[]{:S(2)}) collective-permute-start(bf16[16,9344]{1,0:T(8,128)(2,1)} %get-tuple-element.139), channel_id=1, source_target_pairs={{0,8},{4,12},{8,0},{12,4},{1,9},{5,13},{9,1},{13,5},{2,10},{6,14},... | collective-permute-start | bytes 897032 | tf_op jit(solution)/shard_map/ppermute | solution.py:350
  281.1 38.6 %collective-permute-start.7 = (bf16[16,9344]{1,0:T(8,128)(2,1)}, bf16[16,9344]{1,0:T(8,128)(2,1)S(1)}, u32[]{:S(2)}, u32[]{:S(2)}) collective-permute-start(bf16[16,9344]{1,0:T(8,128)(2,1)} %get-tuple-element.140), channel_id=1, source_target_pairs={{0,12},{4,8},{8,4},{12,0},{1,13},{5,9},{9,5},{13,1},{2,14},{6,10},... | collective-permute-start | bytes 897032 | tf_op jit(solution)/shard_map/ppermute | solution.py:350
  321.1 8.1 %copy-start.1 = (f32[8,128,128]{2,1,0:T(8,128)S(1)}, f32[8,128,128]{2,1,0:T(8,128)}, u32[]{:S(2)}) copy-start(f32[8,128,128]{2,1,0:T(8,128)} %param.22) | copy-start | bytes 1572868
  (9 other events, 14.9 us)

commit v2 on v1

--- a/solution.py
+++ b/solution.py
@@ -16,10 +16,13 @@
 PAIR_LANES = 2 * NG
 ROWS = 16
 NEAR = 2
+UNROLL = 4
 
 PRECISE = lax.Precision.HIGHEST
 SPACING = 0.1348
-VMEM_BYTES = 56 * 1024 * 1024
+VMEM_BYTES = 32 * 1024 * 1024
+TILE_VMEM_BYTES = 16 * 1024 * 1024
+VMEM_FIRST = 56 * 1024 * 1024
 
 
 def signed_freq(position, length):
@@ -83,7 +86,7 @@
     return both[:count] + both[count:]
 
 
-def forward_kernel(slab, pen, meta_ref, left_ref, right_ref, depth_ref, cols_ref, *refs):
+def forward_kernel(slab, pen, pairs_ref, left_ref, right_ref, depth_ref, cols_ref, *refs):
     outs, (rows_ref, head_ref, tail_ref, rest_ref) = refs[-4 - pen : -4], refs[-4:]
     half = NG // 2
     chunk = 32
@@ -135,9 +138,9 @@
         tail_ref[pl.ds(plane, half, stride=ROWS), :] = rounded(jnp.concatenate(tails, axis=0), pl.ds(NG, half))
         return carry
 
-    lax.fori_loop(0, ROWS, cols_step, 0, unroll=4)
+    lax.fori_loop(0, ROWS, cols_step, 0, unroll=UNROLL)
     for s in range(pen):
-        owner = meta_ref[2] ^ s
+        owner = lax.axis_index("pen") ^ s
         for r in range(slab):
             place = pl.ds(pl.multiple_of((owner * slab + r) * ROWS, ROWS), ROWS)
             outs[s][:, r * LANE : (r + 1) * LANE] = head_ref[place, :].astype(jnp.bfloat16)
@@ -146,18 +149,23 @@
             outs[s][:, (slab + r) * LANE : (slab + r + 1) * LANE] = tail_ref[place, :].astype(jnp.bfloat16)
 
 
-def middle_kernel(pen, in_pieces, out_pieces, extra, meta_ref, table_ref, grid_ref, part_ref, *refs):
+def middle_kernel(pen, in_pieces, out_pieces, extra, in_ref, out_table_ref, grid_ref, part_ref, *refs):
     fields, outs, planes_ref = refs[: len(in_pieces)], refs[len(in_pieces) : -1], refs[-1]
     slab = NG // pen
     block = planes_ref.shape[1]
 
     def place(s, first, count):
-        return pl.ds(pl.multiple_of((meta_ref[2] ^ s) * slab + first, ROWS), count)
+        return pl.ds(pl.multiple_of((lax.axis_index("pen") ^ s) * slab + first, ROWS), count)
 
     for field, piece in zip(fields, in_pieces):
         planes_ref[place(*piece), :] = field[...]
-    spectral = stacked_dot_exact(table_ref[...], planes_ref[...]) * grid_ref[...]
-    planes_ref[...] = stacked_dot(table_ref[...], spectral).astype(jnp.bfloat16)
+    half = NG // 2
+    weights = grid_ref[:half, :]
+    top = lax.broadcasted_iota(jnp.int32, (ROWS // 2, block), 0) == 0
+    mirrored = jnp.where(top, grid_ref[half:, :], weights[: ROWS // 2])
+    weights = jnp.concatenate([weights, mirrored, weights[ROWS // 2 :]], axis=0)
+    spectral = stacked_dot_exact(in_ref[...], planes_ref[...]) * weights
+    planes_ref[...] = stacked_dot(out_table_ref[...], spectral).astype(jnp.bfloat16)
     for out_ref, piece in zip(outs, out_pieces):
         values = planes_ref[place(*piece), :]
         if not (extra and piece[1] + piece[2] == slab):
@@ -165,7 +173,7 @@
             continue
         lanes = pl.ds(pl.multiple_of(pl.program_id(0) * block, LANE), block)
         out_ref[:, lanes] = values
-        high, rest = split_rest(part_ref[meta_ref[2] ^ piece[0]])
+        high, rest = split_rest(part_ref[lax.axis_index("pen") ^ piece[0]])
         middle, rest = split_rest(rest)
         blank = jnp.zeros((ROWS - 3 * high.shape[0], LANE), jnp.float32)
         if piece[2] > ROWS:
@@ -174,7 +182,7 @@
         out_ref[piece[2] - ROWS :, width_of(slab) :] = tag
 
 
-def inverse_kernel(slab, pen, extra, meta_ref, *refs):
+def inverse_kernel(slab, pen, extra, pairs_ref, *refs):
     fields = refs[:pen]
     right_ref, cols_ref, depth_ref = refs[pen : pen + 3]
     out_ref, rows_ref, head_ref, tail_ref = refs[-4:]
@@ -186,7 +194,7 @@
     half = NG // 2
     chunk = 32
     for s in range(pen):
-        owner = meta_ref[2] ^ s
+        owner = lax.axis_index("pen") ^ s
         for r in range(slab):
             place = pl.ds(pl.multiple_of((owner * slab + r) * ROWS, ROWS), ROWS)
             head_ref[place, :] = fields[s][:, r * LANE : (r + 1) * LANE].astype(jnp.float32)
@@ -209,7 +217,7 @@
         rows_ref[1, strided, :] = result[:, LANE:]
         return carry
 
-    lax.fori_loop(0, ROWS, cols_step, 0, unroll=4)
+    lax.fori_loop(0, ROWS, cols_step, 0, unroll=UNROLL)
 
     def depth_step(step, carry):
         results = []
@@ -227,6 +235,47 @@
     lax.fori_loop(0, half // chunk, depth_step, 0)
 
 
+def fit_kernel(aux_ref, slots_ref, count_ref, tiles_ref, density_ref, gamma_ref, rows_ref):
+    rows_ref[...] = density_ref[...].astype(jnp.float32)
+    gamma_ref[...] = jnp.zeros_like(gamma_ref)
+    base = lax.axis_index("pen") * gamma_ref.shape[0]
+    for t in range(tiles_ref.shape[0]):
+        row = jnp.broadcast_to(rows_ref[pl.ds(slots_ref[t], 1), :], (ROWS, LANE)).astype(jnp.bfloat16)
+        value = lax.dot_general(row, tiles_ref[t], (((1,), (1,)), ((), ())), preferred_element_type=jnp.float32)
+        place = pl.ds(aux_ref[t] - base, 1)
+        gamma_ref[place, :] += jnp.where(t < count_ref[0], value[:1], 0.0)
+
+
+def build_kernel(aux_ref, slots_ref, count_ref, tiles_ref, coef_ref, part_ref):
+    part_ref[...] = jnp.zeros_like(part_ref)
+    base = lax.axis_index("pen") * coef_ref.shape[0]
+    for t in range(tiles_ref.shape[0]):
+        row = jnp.broadcast_to(coef_ref[pl.ds(aux_ref[t] - base, 1), :], (ROWS, LANE)).astype(jnp.bfloat16)
+        value = dot32(row, tiles_ref[t])
+        place = pl.ds(slots_ref[t], 1)
+        part_ref[place, :] += jnp.where(t < count_ref[0], value[:1], 0.0)
+
+
+def tile_call(kernel, tiles, rows, out_rows, scratch, name):
+    tile_blocks, tile_aux, tile_pair, tile_count = tiles
+    return pl.pallas_call(
+        kernel,
+        out_shape=jax.ShapeDtypeStruct((out_rows, LANE), jnp.float32),
+        grid_spec=pltpu.PrefetchScalarGridSpec(
+            num_scalar_prefetch=3,
+            grid=(1,),
+            in_specs=[whole_spec(tile_blocks.shape), whole_spec(rows.shape)],
+            out_specs=whole_spec((out_rows, LANE)),
+            scratch_shapes=scratch,
+        ),
+        compiler_params=pltpu.CompilerParams(vmem_limit_bytes=TILE_VMEM_BYTES),
+        cost_estimate=pl.CostEstimate(
+            flops=2 * tile_blocks.size * ROWS, bytes_accessed=2 * tile_blocks.size, transcendentals=0
+        ),
+        name=name,
+    )(tile_aux, tile_pair, tile_count, tile_blocks, rows)
+
+
 def whole_spec(shape):
     return pl.BlockSpec(shape, lambda *_: (0,) * len(shape))
 
@@ -239,13 +288,13 @@
     ]
 
 
-def forward_planes(meta, orbitals, depth_tables, cols_table, pen, first, count, earlier, after):
+def forward_planes(pair_index, pair, orbitals, depth_tables, cols_table, pen, first, count, earlier, after):
     slab = NG // pen
     width = width_of(slab)
     skip = first // ROWS
     near = jax.ShapeDtypeStruct((slab, width), jnp.bfloat16)
     far = jax.ShapeDtypeStruct((count, width), jnp.bfloat16)
-    operands = [meta, orbitals, orbitals, depth_tables, cols_table]
+    operands = [pair_index, orbitals, orbitals, depth_tables, cols_table]
     aliases = {len(operands) + s: s for s in range(len(earlier))}
     operands += [*earlier, *after]
     return pl.pallas_call(
@@ -255,18 +304,18 @@
             num_scalar_prefetch=1,
             grid=(count // ROWS,),
             in_specs=[
-                pl.BlockSpec((1, ROWS, NG * NG), lambda b, meta: (meta[0], b + skip, 0)),
-                pl.BlockSpec((1, ROWS, NG * NG), lambda b, meta: (meta[1], b + skip, 0)),
+                pl.BlockSpec((1, ROWS, NG * NG), lambda b, pairs: (pairs[pair, 0], b + skip, 0)),
+                pl.BlockSpec((1, ROWS, NG * NG), lambda b, pairs: (pairs[pair, 1], b + skip, 0)),
                 whole_spec(depth_tables.shape),
                 whole_spec(cols_table.shape),
             ]
             + [pl.BlockSpec(memory_space=pl.ANY)] * (len(earlier) + len(after)),
-            out_specs=[pl.BlockSpec((ROWS, width), lambda b, meta: (b + skip, 0))] * NEAR
-            + [pl.BlockSpec((ROWS, width), lambda b, meta: (b, 0))] * (pen - NEAR),
+            out_specs=[pl.BlockSpec((ROWS, width), lambda b, *_: (b + skip, 0))] * NEAR
+            + [pl.BlockSpec((ROWS, width), lambda b, *_: (b, 0))] * (pen - NEAR),
             scratch_shapes=column_scratch() + [pltpu.VMEM((NG + NG // 2, LANE), jnp.float32)],
         ),
         input_output_aliases=aliases,
-        compiler_params=pltpu.CompilerParams(vmem_limit_bytes=VMEM_BYTES),
+        compiler_params=pltpu.CompilerParams(vmem_limit_bytes=VMEM_BYTES if earlier else VMEM_FIRST),
         cost_estimate=pl.CostEstimate(
             flops=2 * 6 * count * NG * NG * NG, bytes_accessed=6 * count * NG * NG, transcendentals=0
         ),
@@ -274,7 +323,7 @@
     )(*operands)
 
 
-def middle_columns(meta, fields, in_pieces, table, grid_table, part, pen, out_pieces, extra):
+def middle_columns(fields, in_pieces, tables, grid_table, part, pen, out_pieces, extra):
     slab = NG // pen
     width = width_of(slab)
     block = width // 8
@@ -285,43 +334,41 @@
             out_specs.append(whole_spec((count, width + LANE)))
         else:
             out_shapes.append(jax.ShapeDtypeStruct((count, width), jnp.bfloat16))
-            out_specs.append(pl.BlockSpec((count, block), lambda b, meta: (0, b)))
-    in_specs = [whole_spec(table.shape), pl.BlockSpec((NG, block), lambda b, meta: (0, b)), whole_spec(part.shape)]
-    in_specs += [pl.BlockSpec((count, block), lambda b, meta: (0, b)) for s, first, count in in_pieces]
+            out_specs.append(pl.BlockSpec((count, block), lambda b, *_: (0, b)))
+    in_specs = [whole_spec(table.shape) for table in tables]
+    in_specs += [pl.BlockSpec((grid_table.shape[0], block), lambda b, *_: (0, b)), whole_spec(part.shape)]
+    in_specs += [pl.BlockSpec((count, block), lambda b, *_: (0, b)) for s, first, count in in_pieces]
     return pl.pallas_call(
         functools.partial(middle_kernel, pen, in_pieces, out_pieces, extra),
         out_shape=out_shapes,
-        grid_spec=pltpu.PrefetchScalarGridSpec(
-            num_scalar_prefetch=1,
-            grid=(width // block,),
-            in_specs=in_specs,
-            out_specs=out_specs,
-            scratch_shapes=[pltpu.VMEM((NG, block), jnp.bfloat16)],
-        ),
+        grid=(width // block,),
+        in_specs=in_specs,
+        out_specs=out_specs,
+        scratch_shapes=[pltpu.VMEM((NG, block), jnp.bfloat16)],
         compiler_params=pltpu.CompilerParams(vmem_limit_bytes=VMEM_BYTES),
         cost_estimate=pl.CostEstimate(flops=2 * 5 * NG * NG * width, bytes_accessed=8 * NG * width, transcendentals=0),
         name="middle_columns",
-    )(meta, table, grid_table, part, *fields)
-
-
-def inverse_planes(meta, fields, orbitals, cols_table, depth_tables, pair, pairs, first, earlier, part_rows):
+    )(*tables, grid_table, part, *fields)
+
+
+def inverse_planes(pair_index, pair, fields, orbitals, cols_table, depth_tables, first, earlier, part_rows):
     pen = len(fields)
     slab = NG // pen
     count = fields[-1].shape[0]
     skip = first // ROWS
-    out_shapes = [jax.ShapeDtypeStruct((pairs, slab, NG * NG), jnp.float32)]
-    out_specs = [pl.BlockSpec((1, ROWS, NG * NG), lambda b, meta: (pair, b + skip, 0))]
+    out_shapes = [jax.ShapeDtypeStruct((pair_index.shape[0], slab, NG * NG), jnp.float32)]
+    out_specs = [pl.BlockSpec((1, ROWS, NG * NG), lambda b, *_: (pair, b + skip, 0))]
     if part_rows:
         out_shapes.append(jax.ShapeDtypeStruct((part_rows, LANE), jnp.float32))
         out_specs.append(whole_spec((part_rows, LANE)))
-    in_specs = [pl.BlockSpec((ROWS, field.shape[1]), lambda b, meta: (b + skip, 0)) for field in fields[:NEAR]]
-    in_specs += [pl.BlockSpec((ROWS, field.shape[1]), lambda b, meta: (b, 0)) for field in fields[NEAR:]]
+    in_specs = [pl.BlockSpec((ROWS, field.shape[1]), lambda b, *_: (b + skip, 0)) for field in fields[:NEAR]]
+    in_specs += [pl.BlockSpec((ROWS, field.shape[1]), lambda b, *_: (b, 0)) for field in fields[NEAR:]]
     in_specs += [
-        pl.BlockSpec((1, ROWS, NG * NG), lambda b, meta: (meta[1], b + skip, 0)),
+        pl.BlockSpec((1, ROWS, NG * NG), lambda b, pairs: (pairs[pair, 1], b + skip, 0)),
         whole_spec(cols_table.shape),
         whole_spec(depth_tables.shape),
     ]
-    operands = [meta, *fields, orbitals, cols_table, depth_tables]
+    operands = [pair_index, *fields, orbitals, cols_table, depth_tables]
     aliases = {}
     if earlier is not None:
         aliases = {len(operands): 0}
@@ -374,9 +421,15 @@
     tail_depth = jnp.broadcast_to(LANE + lane % TAIL, tail_col.shape)
     col = signed_freq(me * slab + jnp.concatenate([head_col, tail_col], axis=0).reshape(-1), NG)
     depth = signed_freq(jnp.concatenate([head_depth, tail_depth], axis=0).reshape(-1), NG)
-    plane = signed_freq(jnp.arange(NG, dtype=jnp.int32), NG)
+    plane = jnp.arange(NG // 2 + ROWS // 2, dtype=jnp.int32)
     square_sum = (plane * plane)[:, None] + (col * col + depth * depth)[None, :]
     return coulomb_kernel(square_sum, NG) / float(NG * NG * NG)
+
+
+def plane_frequencies():
+    upper = (NG - np.arange(NG // 2)) % NG
+    upper[0] = NG // 2
+    return np.concatenate([np.arange(NG // 2), upper])
 
 
 def plane_runs(slab, first, last):
@@ -392,7 +445,7 @@
     return far + tuple((s, 0, NG // pen) for s in range(NEAR - 1, -1, -1))
 
 
-def both_parts(orbitals, pair_index, pen, coulomb_part):
+def both_parts(orbitals, pair_index, pen, coulomb_local, coulomb_part):
     slab = NG // pen
     pairs = pair_index.shape[0]
     me = lax.axis_index("pen").astype(jnp.int32)
@@ -402,8 +455,11 @@
     depth_tables, depth_back = jnp.asarray(depth_np), jnp.asarray(np.swapaxes(depth_np, 2, 3))
     cols_forward = jnp.asarray(stack_split(cas_table(positions[:, None], interleaved[None, :])))
     cols_back = jnp.asarray(stack_split(cas_table(interleaved[:, None], positions[None, :])))
-    plane_table = jnp.asarray(stack_split(cas_table(positions[:, None], positions[None, :])))
-    metas = [jnp.concatenate([pair_index[p], me[None]]) for p in range(pairs)]
+    frequencies = plane_frequencies()
+    plane_tables = (
+        jnp.asarray(stack_split(cas_table(frequencies[:, None], positions[None, :]))),
+        jnp.asarray(stack_split(cas_table(positions[:, None], frequencies[None, :]))),
+    )
 
     held, after = [], []
     for p in range(pairs):
@@ -411,20 +467,21 @@
         taken, made = {}, ()
         for first, count in runs:
             made = forward_planes(
-                metas[p], orbitals, depth_tables, cols_forward, pen, first, count, made[:NEAR], after if first == 0 else ()
+                pair_index, p, orbitals, depth_tables, cols_forward, pen, first, count, made[:NEAR], after if first == 0 else ()
             )
             for s in range(NEAR, pen):
                 taken[s, first] = exchange(s, made[s], pen)
+            if p == 0 and first == 0:
+                local = coulomb_local(made[-1])
         for s in range(NEAR):
             taken[s, 0] = exchange(s, made[s], pen)
         pieces = pieces_of(pen, runs)
         held.append((pieces, [taken[s, first] for s, first, count in pieces]))
         if p == 0:
-            local, part_of = coulomb_part(made[-1])
-            after = [local] + [taken[s, 0] for s in range(NEAR, pen) if len(runs) > 1]
-    late_me, _ = lax.optimization_barrier((me, made[-1]))
-    grid_table = grid_weights(late_me, slab)
-    part = part_of(local)
+            late_me, _ = lax.optimization_barrier((me, made[-1]))
+            grid_table = grid_weights(late_me, slab)
+            after = [grid_table, local]
+    part = coulomb_part(local)
 
     back = []
     for p in range(pairs):
@@ -432,7 +489,7 @@
         fed = part if last else jnp.zeros_like(part)
         runs = plane_runs(slab, False, last)
         pieces = pieces_of(pen, runs)
-        filtered = middle_columns(metas[p], held[p][1], held[p][0], plane_table, grid_table, fed, pen, pieces, last)
+        filtered = middle_columns(held[p][1], held[p][0], plane_tables, grid_table, fed, pen, pieces, last)
         back.append((runs, {piece[:2]: exchange(piece[0], field, pen) for piece, field in zip(pieces, filtered)}))
 
     terms = None
@@ -442,7 +499,7 @@
             final = p == pairs - 1 and first + count == slab
             fields = [taken[s, 0 if s < NEAR else first] for s in range(pen)]
             made = inverse_planes(
-                metas[p], fields, orbitals, cols_back, depth_back, p, pairs, first, terms, part.shape[1] if final else 0
+                pair_index, p, fields, orbitals, cols_back, depth_back, first, terms, part.shape[1] if final else 0
             )
             terms = made[0]
     return made[1], terms
@@ -498,6 +555,11 @@
     return lax.fori_loop(0, block_count, add_block, initial)
 
 
+def to_all(values, count, axes):
+    copies = jnp.broadcast_to(values[None], (count, *values.shape))
+    return lax.all_to_all(copies, axes, split_axis=0, concat_axis=0, tiled=True)
+
+
 def coulomb_partial(tile_blocks, tile_aux, tile_pair, tile_count, density, metric_inv):
     aux_count = metric_inv.shape[0]
     dens_all = lax.all_gather(density, "blk", axis=0, tiled=True)
@@ -535,17 +597,23 @@
     tiles = (tile_blocks, tile_aux, tile_pair, tile_count)
     if slab % ROWS == 0 and pen & (pen - 1) == 0 and pen >= NEAR and rows <= ROWS // 3:
 
-        def coulomb_part(after):
+        def coulomb_local(after):
             late_density, _ = lax.optimization_barrier((density, after))
-            return coulomb_partial(*tiles, late_density, metric_inv), sum_part
-
-        def sum_part(local):
+            dens_all = to_all(late_density, blk, "blk").reshape(-1, LANE)
+            scratch = [pltpu.VMEM(dens_all.shape, jnp.float32)]
+            gamma = tile_call(fit_kernel, tiles, dens_all, metric_inv.shape[0], scratch, "fit_tiles")
+            gamma = to_all(gamma, grp * blk, ("grp", "blk")).sum(axis=0)
+            coef = jnp.einsum("kab,kb->ka", metric_inv, gamma, precision=PRECISE)
+            coef = lax.reduce_precision(coef, 8, 7)
+            return tile_call(build_kernel, tiles, coef, dens_all.shape[0], [], "build_tiles")
+
+        def coulomb_part(local):
             shares = local.reshape(grp, pen, blk, rows, LANE).transpose(0, 2, 1, 3, 4)
             shares = shares.reshape(grp * blk, pen * rows, LANE)
             taken = lax.all_to_all(shares, ("grp", "blk"), split_axis=0, concat_axis=0, tiled=True)
             return taken.sum(axis=0).reshape(pen, rows, LANE)
 
-        return both_parts(orbitals, pair_index, pen, coulomb_part)
+        return both_parts(orbitals, pair_index, pen, coulomb_local, coulomb_part)
     part = coulomb_partial(*tiles, density, metric_inv)
     coulomb = lax.psum_scatter(part, ("grp", "pen", "blk"), scatter_dimension=0, tiled=True)
     return coulomb, pair_fields_plain(orbitals, pair_index, pen)

time: 330 us -> 324 us (0.982)
  waiting for transfers between devices: 120 us -> 159 us
  blocking collectives: 32.7 us -> 8.45 us
  other arithmetic: 34.2 us -> 15.7 us
  Pallas kernels: 102 us -> 96.1 us
    ppermute x16, waiting for transfers between devices: 120 us -> 159 us  [exchange(): lax.ppermute(field, 'pen', [(i, i ^ s) for i in range(pen)])]
    psum x1 -> x0, blocking collectives: 17.2 us -> none  [coulomb_partial(): gamma_all = lax.psum(gamma, ('grp', 'blk'))]
    div x1, other arithmetic: 27.8 us -> 15.6 us  [grid_weights(): return coulomb_kernel(square_sum, NG) / float(NG * NG * NG)]
    all_gather x1 -> x0, blocking collectives: 8.19 us -> none  [coulomb_partial(): dens_all = lax.all_gather(density, 'blk', axis=0, tiled=True)]
    all_to_all x0 -> x2, starting transfers between devices: none -> 7.92 us  [to_all(): return lax.all_to_all(copies, axes, split_axis=0, concat_axis=0, tiled=True)]
    pallas_call x2, Pallas kernels: 24.8 us -> 19.4 us  [middle_columns(): pl.pallas_call(functools.partial(middle_kernel, pen, in_pieces, out_piece...]
    ppermute x16, starting transfers between devices: 29.6 us -> 24.2 us  [exchange(): lax.ppermute(field, 'pen', [(i, i ^ s) for i in range(pen)])]
    unnamed x34 -> x48, local copies, waits for them, and re-layouts: 4.32 us -> 8.07 us
  transfers between devices with their start and end apart: 16 -> 18, of which waited for: 5 -> 6; matrix products, arithmetic and copies ran while one was open for 12% -> 6% of each run, Pallas kernels for 26% -> 25%
where the time goes in v2:
time: 324 us; the launch traced here: 323 us
  waiting for transfers between devices  159 us (49%)
  Pallas kernels  96.1 us (30%)
  starting transfers between devices  32.1 us (10%)
  other arithmetic  15.7 us (5%)
  local copies, waits for them, and re-layouts  9.33 us (3%)
  blocking collectives  8.45 us (3%)
    ppermute x16, waiting for transfers between devices, exchange(): lax.ppermute(field, 'pen', [(i, i ^ s) for i in range(pen)])  159 us
    pallas_call x3, Pallas kernels, forward_planes(): pl.pallas_call(functools.partial(forward_kernel, slab, pen), out_shape=[n...  40.4 us
    pallas_call x3, Pallas kernels, inverse_planes(): pl.pallas_call(functools.partial(inverse_kernel, slab, pen, bool(part_row...  34.1 us
    ppermute x16, starting transfers between devices, exchange(): lax.ppermute(field, 'pen', [(i, i ^ s) for i in range(pen)])  24.2 us
    pallas_call x2, Pallas kernels, middle_columns(): pl.pallas_call(functools.partial(middle_kernel, pen, in_pieces, out_piece...  19.4 us
    div x1, other arithmetic, grid_weights(): return coulomb_kernel(square_sum, NG) / float(NG * NG * NG)  15.6 us
    all_to_all x1, blocking collectives, coulomb_part(): lax.all_to_all(shares, ('grp', 'blk'), split_axis=0, concat_axis=0, tiled...  8.45 us
    unnamed x48, local copies, waits for them, and re-layouts  8.07 us
  transfers between devices with their start and end apart: 18, of which 6 were waited for; matrix products, arithmetic and copies ran while one was open for 6% of the time, Pallas kernels for 25%

profile of v2, /device:TPU:8, one launch (start us, length us, event | category | flops | bytes accessed | tf_op | source)
XLA Modules:
  0.0 323.0 jit_solution(15270492477245423955)
XLA Ops:
  0.7 8.5 %forward_planes.3 = (bf16[48,9216]{1,0:T(8,128)(2,1)}, bf16[48,9216]{1,0:T(8,128)(2,1)}, bf16[16,9216]{1,0:T(8,128)(2,1)}, bf16[16,9216]{1,0:T(8,128)(2,1)}) custom-call(s32[2,2]{1,0:T(2,128)} %pairs_ref.11, bf16[8,48,36864]{2,1,0:T(8,128)(2,1)} %refs_4_.5, bf16[8,48,36864]{2,1,0:T(8,128)(2,1)} %refs_4_.5, ...), custom_call_target="tpu_custom_call" | custom-call | flops 1358954496 | bytes 3538944 | tf_op jit(solution)/shard_map/forward_planes/pallas_call | solution.py:300
  11.4 3.7 %all-to-all-start = ((bf16[4,32,128]{2,1,0:T(8,128)(2,1)}), bf16[4,32,128]{2,1,0:T(8,128)(2,1)S(1)}, u32[]{:S(2)}, u32[]{:S(2)}) async-start(bf16[4,32,128]{2,1,0:T(8,128)(2,1)} %broadcast_in_dim.76), calls=%async_computation | async-start | bytes 65536 | tf_op jit(solution)/shard_map/all_to_all | solution.py:560
  17.5 13.0 %forward_planes.4 = (bf16[48,9216]{1,0:T(8,128)(2,1)S(1)}, bf16[48,9216]{1,0:T(8,128)(2,1)}, bf16[32,9216]{1,0:T(8,128)(2,1)}, bf16[32,9216]{1,0:T(8,128)(2,1)}) custom-call(s32[2,2]{1,0:T(2,128)S(1)} %copy-done.14, bf16[8,48,36864]{2,1,0:T(8,128)(2,1)} %refs_4_.5, bf16[8,48,36864]{2,1,0:T(8,128)(2,1)} %refs_4_.5, ...), custom_call_target="tpu_custom_call", output_to_operand_aliasing={{0}: (5, {}), {1}: (6, {})} | custom-call | flops 2717908992 | bytes 7077888 | tf_op jit(solution)/shard_map/forward_planes/pallas_call | solution.py:300
  31.5 1.7 collective-permute-start.11
  38.5 4.2 %all-to-all-start.1 = ((f32[8,8,128]{2,1,0:T(8,128)}), f32[8,8,128]{2,1,0:T(8,128)S(1)}, u32[]{:S(2)}, u32[]{:S(2)}) async-start(f32[8,8,128]{2,1,0:T(8,128)} %broadcast_in_dim.77), calls=%async_computation.1 | async-start | bytes 65536 | tf_op jit(solution)/shard_map/all_to_all | solution.py:560
  42.7 15.6 %fusion.3.refs_0_.grid_ref = f32[104,9216]{1,0:T(8,128)} fusion(s32[9216]{0:T(1024)S(1)} %fusion.10, s32[104]{0:T(128)S(1)} %iota_multiply_fusion), kind=kLoop, calls=%fused_computation.5 | loop fusion | flops 9584640 | bytes 3871136 | tf_op jit(solution)/shard_map/div | solution.py:426
  60.8 18.9 %forward_planes.5 = (bf16[48,9216]{1,0:T(8,128)(2,1)}, bf16[48,9216]{1,0:T(8,128)(2,1)}, bf16[48,9216]{1,0:T(8,128)(2,1)}, bf16[48,9216]{1,0:T(8,128)(2,1)}) custom-call(s32[2,2]{1,0:T(2,128)} %pairs_ref.11, bf16[8,48,36864]{2,1,0:T(8,128)(2,1)} %refs_4_.5, bf16[8,48,36864]{2,1,0:T(8,128)(2,1)} %refs_4_.5, ...), custom_call_target="tpu_custom_call" | custom-call | flops 4076863488 | bytes 10616832 | tf_op jit(solution)/shard_map/forward_planes/pallas_call | solution.py:300
  79.7 2.8 collective-permute-start
  84.1 42.6 %collective-permute-done.10.refs_2_ = bf16[32,9216]{1,0:T(8,128)(2,1)} collective-permute-done((bf16[32,9216]{1,0:T(8,128)(2,1)}, bf16[32,9216]{1,0:T(8,128)(2,1)}, u32[]{:S(2)}, u32[]{:S(2)}) %collective-permute-start.10) | collective-permute-done | bytes 589856 | tf_op jit(solution)/shard_map/ppermute | solution.py:397
  126.8 10.1 %middle_columns.3 = (bf16[48,9216]{1,0:T(8,128)(2,1)S(1)}, bf16[48,9216]{1,0:T(8,128)(2,1)S(1)}, bf16[48,9216]{1,0:T(8,128)(2,1)}, bf16[48,9216]{1,0:T(8,128)(2,1)S(1)}) custom-call(bf16[384,192]{1,0:T(8,128)(2,1)S(1)} %copy-done.22, bf16[384,192]{1,0:T(8,128)(2,1)S(1)} %copy-done.21, f32[104,9216]{1,0:T(8,128)S(1)} %copy-done.2, ...), custom_call_target="tpu_custom_call" | custom-call | flops 3397386240 | bytes 14155776 | tf_op jit(solution)/shard_map/middle_columns/pallas_call | solution.py:341
  138.9 8.4 %all_to_all.15 = f32[8,16,128]{2,1,0:T(8,128)S(1)} all-to-all(f32[8,16,128]{2,1,0:T(8,128)S(1)} %bitcast.28), channel_id=1, replica_groups=mesh['grp'=2,'pen'=4,'blk'=4] {'grp','blk'}, dimensions={0} | all-to-all | bytes 131072 | tf_op jit(solution)/shard_map/all_to_all | solution.py:613
  147.4 3.3 %collective-permute-start.14 = (bf16[48,9216]{1,0:T(8,128)(2,1)}, bf16[48,9216]{1,0:T(8,128)(2,1)S(1)}, u32[]{:S(2)}, u32[]{:S(2)}) collective-permute-start(bf16[48,9216]{1,0:T(8,128)(2,1)} %copy-done.20), channel_id=1, source_target_pairs={{0,8},{4,12},{8,0},{12,4},{1,9},{5,13},{9,1},{13,5},{2,10},{6,14},... | collective-permute-start | bytes 2654216 | tf_op jit(solution)/shard_map/ppermute | solution.py:397
  150.9 51.0 %collective-permute-done.1.refs_1_ = bf16[48,9216]{1,0:T(8,128)(2,1)} collective-permute-done((bf16[48,9216]{1,0:T(8,128)(2,1)}, bf16[48,9216]{1,0:T(8,128)(2,1)}, u32[]{:S(2)}, u32[]{:S(2)}) %collective-permute-start.1) | collective-permute-done | bytes 884768 | tf_op jit(solution)/shard_map/ppermute | solution.py:397
  201.9 2.1 copy-done.3
  205.1 9.3 %middle_columns.2 = (bf16[32,9216]{1,0:T(8,128)(2,1)S(1)}, bf16[32,9216]{1,0:T(8,128)(2,1)S(1)}, bf16[16,9344]{1,0:T(8,128)(2,1)S(1)}, bf16[16,9344]{1,0:T(8,128...) custom-call(bf16[384,192]{1,0:T(8,128)(2,1)S(1)} %copy-done.22, bf16[384,192]{1,0:T(8,128)(2,1)S(1)} %copy-done.21, ...), custom_call_target="tpu_custom_call" | custom-call | flops 3397386240 | bytes 14155776 | tf_op jit(solution)/shard_map/middle_columns/pallas_call | solution.py:341
  214.5 2.3 collective-permute-start.3
  218.5 2.3 collective-permute-done.14.refs_2_
  220.9 3.3 %collective-permute-start.4 = (bf16[16,9344]{1,0:T(8,128)(2,1)S(1)}, bf16[16,9344]{1,0:T(8,128)(2,1)S(1)}, u32[]{:S(2)}, u32[]{:S(2)}) collective-permute-start(bf16[16,9344]{1,0:T(8,128)(2,1)S(1)} %get-tuple-element.40), channel_id=1, source_target_pairs={{0,8},{4,12},{8,0},{12,4},{1,9},{5,13},{9,1},{13,5},{2,10},{6,14},... | collective-permute-start | bytes 897032 | tf_op jit(solution)/shard_map/ppermute | solution.py:397
  224.2 54.4 %collective-permute-done.15.refs_3_ = bf16[48,9216]{1,0:T(8,128)(2,1)S(1)} collective-permute-done((bf16[48,9216]{1,0:T(8,128)(2,1)}, bf16[48,9216]{1,0:T(8,128)(2,1)S(1)}, u32[]{:S(2)}, u32[]{:S(2)}) %collective-permute-start.15) | collective-permute-done | bytes 884768 | tf_op jit(solution)/shard_map/ppermute | solution.py:397
  278.5 1.8 collective-permute-start.5
  280.3 15.4 %inverse_planes.3.refs_7_ = f32[2,48,36864]{2,1,0:T(8,128)} custom-call(s32[2,2]{1,0:T(2,128)S(1)} %copy-done.15, bf16[48,9216]{1,0:T(8,128)(2,1)S(1)} %get-tuple-element.48.refs_0_, bf16[48,9216]{1,0:T(8,128)(2,1)S(1)} %collective-permute-done.13.refs_1_, bf16[48,9216]{1,0:T(8,128)(2,1)S(1)} %collective-permute-done.14.refs_2_, ...), custom_call_target="tpu_custom_call" | custom-call | flops 3397386240 | bytes 14155776 | tf_op jit(solution)/shard_map/inverse_planes/pallas_call | solution.py:377
  295.7 8.1 %collective-permute-done.7.refs_3_ = bf16[32,9216]{1,0:T(8,128)(2,1)S(1)} collective-permute-done((bf16[32,9216]{1,0:T(8,128)(2,1)S(1)}, bf16[32,9216]{1,0:T(8,128)(2,1)S(1)}, u32[]{:S(2)}, u32[]{:S(2)}) %collective-permute-start.7) | collective-permute-done | bytes 589856 | tf_op jit(solution)/shard_map/ppermute | solution.py:397
  303.8 11.4 %inverse_planes.4.refs_7_ = f32[2,48,36864]{2,1,0:T(8,128)} custom-call(s32[2,2]{1,0:T(2,128)S(1)} %copy-done.15, bf16[48,9344]{1,0:T(8,128)(2,1)S(1)} %get-tuple-element.38.refs_0_, bf16[48,9344]{1,0:T(8,128)(2,1)S(1)} %collective-permute-done.3.refs_1_, bf16[32,9216]{1,0:T(8,128)(2,1)S(1)} %collective-permute-done.6.refs_2_, ...), custom_call_target="tpu_custom_call", output_to_operand_aliasing={{}: (8, {})} | custom-call | flops 2264924160 | bytes 9437184 | tf_op jit(solution)/shard_map/inverse_planes/pallas_call | solution.py:377
  315.7 7.3 %inverse_planes.5 = (f32[2,48,36864]{2,1,0:T(8,128)}, f32[4,128]{1,0:T(4,128)}) custom-call(s32[2,2]{1,0:T(2,128)S(1)} %copy-done.15, bf16[48,9344]{1,0:T(8,128)(2,1)S(1)} %get-tuple-element.38.refs_0_, bf16[48,9344]{1,0:T(8,128)(2,1)S(1)} %collective-permute-done.3.refs_1_, ...), custom_call_target="tpu_custom_call", output_to_operand_aliasing={{0}: (8, {})} | custom-call | flops 1132462080 | bytes 4718592 | tf_op jit(solution)/shard_map/inverse_planes/pallas_call | solution.py:377
  (90 shorter events, 20.0 us)
Async XLA Ops:
  9.2 73.3 %collective-permute-start.8 = (bf16[16,9216]{1,0:T(8,128)(2,1)}, bf16[16,9216]{1,0:T(8,128)(2,1)S(1)}, u32[]{:S(2)}, u32[]{:S(2)}) collective-permute-start(bf16[16,9216]{1,0:T(8,128)(2,1)} %get-tuple-element.32), channel_id=1, source_target_pairs={{0,12},{4,8},{8,4},{12,0},{1,13},{5,9},{9,5},{13,1},{2,14},{6,10},... | collective-permute-start | bytes 884744 | tf_op jit(solution)/shard_map/ppermute | solution.py:397
  11.4 25.3 %all-to-all-start = ((bf16[4,32,128]{2,1,0:T(8,128)(2,1)}), bf16[4,32,128]{2,1,0:T(8,128)(2,1)S(1)}, u32[]{:S(2)}, u32[]{:S(2)}) async-start(bf16[4,32,128]{2,1,0:T(8,128)(2,1)} %broadcast_in_dim.76), calls=%async_computation | async-start | bytes 65536 | tf_op jit(solution)/shard_map/all_to_all | solution.py:560
  15.1 64.6 %collective-permute-start.9 = (bf16[16,9216]{1,0:T(8,128)(2,1)}, bf16[16,9216]{1,0:T(8,128)(2,1)}, u32[]{:S(2)}, u32[]{:S(2)}) collective-permute-start(bf16[16,9216]{1,0:T(8,128)(2,1)} %get-tuple-element.44), channel_id=1, source_target_pairs={{0,8},{4,12},{8,0},{12,4},{1,9},{5,13},{9,1},{13,5},{2,10},{6,14},... | collective-permute-start | bytes 884744 | tf_op jit(solution)/shard_map/ppermute | solution.py:397
  31.5 51.1 %collective-permute-start.11 = (bf16[32,9216]{1,0:T(8,128)(2,1)}, bf16[32,9216]{1,0:T(8,128)(2,1)}, u32[]{:S(2)}, u32[]{:S(2)}) collective-permute-start(bf16[32,9216]{1,0:T(8,128)(2,1)} %get-tuple-element.45), channel_id=1, source_target_pairs={{0,8},{4,12},{8,0},{12,4},{1,9},{5,13},{9,1},{13,5},{2,10},{6,14},... | collective-permute-start | bytes 1769480 | tf_op jit(solution)/shard_map/ppermute | solution.py:397
  33.2 93.6 %collective-permute-start.10 = (bf16[32,9216]{1,0:T(8,128)(2,1)}, bf16[32,9216]{1,0:T(8,128)(2,1)}, u32[]{:S(2)}, u32[]{:S(2)}) collective-permute-start(bf16[32,9216]{1,0:T(8,128)(2,1)} %get-tuple-element.30), channel_id=1, source_target_pairs={{0,12},{4,8},{8,4},{12,0},{1,13},{5,9},{9,5},{13,1},{2,14},{6,10},... | collective-permute-start | bytes 1769480 | tf_op jit(solution)/shard_map/ppermute | solution.py:397
  34.2 92.5 %collective-permute-start.12 = (bf16[48,9216]{1,0:T(8,128)(2,1)}, bf16[48,9216]{1,0:T(8,128)(2,1)S(1)}, u32[]{:S(2)}, u32[]{:S(2)}) collective-permute-start(bf16[48,9216]{1,0:T(8,128)(2,1)} %get-tuple-element.46), channel_id=1, source_target_pairs={{0,4},{4,0},{8,12},{12,8},{1,5},{5,1},{9,13},{13,9},{2,6},{6,2},{1... | collective-permute-start | bytes 2654216 | tf_op jit(solution)/shard_map/ppermute | solution.py:397
  38.5 19.8 %all-to-all-start.1 = ((f32[8,8,128]{2,1,0:T(8,128)}), f32[8,8,128]{2,1,0:T(8,128)S(1)}, u32[]{:S(2)}, u32[]{:S(2)}) async-start(f32[8,8,128]{2,1,0:T(8,128)} %broadcast_in_dim.77), calls=%async_computation.1 | async-start | bytes 65536 | tf_op jit(solution)/shard_map/all_to_all | solution.py:560
  60.8 65.9 %copy-start.11 = (bf16[48,9216]{1,0:T(8,128)(2,1)S(1)}, bf16[48,9216]{1,0:T(8,128)(2,1)}, u32[]{:S(2)}) copy-start(bf16[48,9216]{1,0:T(8,128)(2,1)} %copy-done.10) | copy-start | bytes 2654212
  60.8 65.9 %copy-start.21 = (bf16[384,192]{1,0:T(8,128)(2,1)S(1)}, bf16[384,192]{1,0:T(8,128)(2,1)}, u32[]{:S(2)}) copy-start(bf16[384,192]{1,0:T(8,128)(2,1)} %constant.67.clone.out_table_ref) | copy-start | bytes 442372
  60.8 65.9 %copy-start.22 = (bf16[384,192]{1,0:T(8,128)(2,1)S(1)}, bf16[384,192]{1,0:T(8,128)(2,1)}, u32[]{:S(2)}) copy-start(bf16[384,192]{1,0:T(8,128)(2,1)} %constant.66.clone.in_ref) | copy-start | bytes 442372
  79.7 70.9 %collective-permute-start = (bf16[48,9216]{1,0:T(8,128)(2,1)}, bf16[48,9216]{1,0:T(8,128)(2,1)}, u32[]{:S(2)}, u32[]{:S(2)}) collective-permute-start(bf16[48,9216]{1,0:T(8,128)(2,1)} %get-tuple-element.34), channel_id=1, source_target_pairs={{0,12},{4,8},{8,4},{12,0},{1,13},{5,9},{9,5},{13,1},{2,14},{6,10},... | collective-permute-start | bytes 2654216 | tf_op jit(solution)/shard_map/ppermute | solution.py:397
  82.5 119.4 %collective-permute-start.1 = (bf16[48,9216]{1,0:T(8,128)(2,1)}, bf16[48,9216]{1,0:T(8,128)(2,1)}, u32[]{:S(2)}, u32[]{:S(2)}) collective-permute-start(bf16[48,9216]{1,0:T(8,128)(2,1)} %get-tuple-element.35), channel_id=1, source_target_pairs={{0,8},{4,12},{8,0},{12,4},{1,9},{5,13},{9,1},{13,5},{2,10},{6,14},... | collective-permute-start | bytes 2654216 | tf_op jit(solution)/shard_map/ppermute | solution.py:397
  82.5 119.3 %collective-permute-start.2 = (bf16[48,9216]{1,0:T(8,128)(2,1)}, bf16[48,9216]{1,0:T(8,128)(2,1)}, u32[]{:S(2)}, u32[]{:S(2)}) collective-permute-start(bf16[48,9216]{1,0:T(8,128)(2,1)} %get-tuple-element.36), channel_id=1, source_target_pairs={{0,4},{4,0},{8,12},{12,8},{1,5},{5,1},{9,13},{13,9},{2,6},{6,2},{1... | collective-permute-start | bytes 2654216 | tf_op jit(solution)/shard_map/ppermute | solution.py:397
  138.9 79.2 %collective-permute-start.13 = (bf16[48,9216]{1,0:T(8,128)(2,1)}, bf16[48,9216]{1,0:T(8,128)(2,1)S(1)}, u32[]{:S(2)}, u32[]{:S(2)}) collective-permute-start(bf16[48,9216]{1,0:T(8,128)(2,1)} %get-tuple-element.49), channel_id=1, source_target_pairs={{0,4},{4,0},{8,12},{12,8},{1,5},{5,1},{9,13},{13,9},{2,6},{6,2},{1... | collective-permute-start | bytes 2654216 | tf_op jit(solution)/shard_map/ppermute | solution.py:397
  147.4 73.5 %collective-permute-start.14 = (bf16[48,9216]{1,0:T(8,128)(2,1)}, bf16[48,9216]{1,0:T(8,128)(2,1)S(1)}, u32[]{:S(2)}, u32[]{:S(2)}) collective-permute-start(bf16[48,9216]{1,0:T(8,128)(2,1)} %copy-done.20), channel_id=1, source_target_pairs={{0,8},{4,12},{8,0},{12,4},{1,9},{5,13},{9,1},{13,5},{2,10},{6,14},... | collective-permute-start | bytes 2654216 | tf_op jit(solution)/shard_map/ppermute | solution.py:397
  150.7 127.9 %collective-permute-start.15 = (bf16[48,9216]{1,0:T(8,128)(2,1)}, bf16[48,9216]{1,0:T(8,128)(2,1)S(1)}, u32[]{:S(2)}, u32[]{:S(2)}) collective-permute-start(bf16[48,9216]{1,0:T(8,128)(2,1)} %copy-done.19), channel_id=1, source_target_pairs={{0,12},{4,8},{8,4},{12,0},{1,13},{5,9},{9,5},{13,1},{2,14},{6,10},... | collective-permute-start | bytes 2654216 | tf_op jit(solution)/shard_map/ppermute | solution.py:397
  205.1 75.2 %copy-start.4 = (bf16[2,2,256,256]{3,2,1,0:T(8,128)(2,1)S(1)}, bf16[2,2,256,256]{3,2,1,0:T(8,128)(2,1)}, u32[]{:S(2)}) copy-start(bf16[2,2,256,256]{3,2,1,0:T(8,128)(2,1)} %constant.63.clone.refs_6_) | copy-start | bytes 1572868
  205.1 75.2 %copy-start.7 = (bf16[384,192]{1,0:T(8,128)(2,1)S(1)}, bf16[384,192]{1,0:T(8,128)(2,1)}, u32[]{:S(2)}) copy-start(bf16[384,192]{1,0:T(8,128)(2,1)} %constant.65.clone.refs_5_) | copy-start | bytes 442372
  205.1 75.2 %copy-start.15 = (s32[2,2]{1,0:T(2,128)S(1)}, s32[2,2]{1,0:T(2,128)}, u32[]{:S(2)}) copy-start(s32[2,2]{1,0:T(2,128)} %pairs_ref.11) | copy-start | bytes 52
  214.5 89.4 %collective-permute-start.3 = (bf16[48,9344]{1,0:T(8,128)(2,1)S(1)}, bf16[48,9344]{1,0:T(8,128)(2,1)S(1)}, u32[]{:S(2)}, u32[]{:S(2)}) collective-permute-start(bf16[48,9344]{1,0:T(8,128)(2,1)S(1)} %get-tuple-element.39), channel_id=1, source_target_pairs={{0,4},{4,0},{8,12},{12,8},{1,5},{5,1},{9,13},{13,9},{2,6},{6,2},{1... | collective-permute-start | bytes 2691080 | tf_op jit(solution)/shard_map/ppermute | solution.py:397
  216.7 79.0 %collective-permute-start.6 = (bf16[32,9216]{1,0:T(8,128)(2,1)S(1)}, bf16[32,9216]{1,0:T(8,128)(2,1)S(1)}, u32[]{:S(2)}, u32[]{:S(2)}) collective-permute-start(bf16[32,9216]{1,0:T(8,128)(2,1)S(1)} %get-tuple-element.42), channel_id=1, source_target_pairs={{0,8},{4,12},{8,0},{12,4},{1,9},{5,13},{9,1},{13,5},{2,10},{6,14},... | collective-permute-start | bytes 1769480 | tf_op jit(solution)/shard_map/ppermute | solution.py:397
  218.0 85.8 %collective-permute-start.7 = (bf16[32,9216]{1,0:T(8,128)(2,1)S(1)}, bf16[32,9216]{1,0:T(8,128)(2,1)S(1)}, u32[]{:S(2)}, u32[]{:S(2)}) collective-permute-start(bf16[32,9216]{1,0:T(8,128)(2,1)S(1)} %get-tuple-element.43), channel_id=1, source_target_pairs={{0,12},{4,8},{8,4},{12,0},{1,13},{5,9},{9,5},{13,1},{2,14},{6,10},... | collective-permute-start | bytes 1769480 | tf_op jit(solution)/shard_map/ppermute | solution.py:397
  220.9 94.3 %collective-permute-start.4 = (bf16[16,9344]{1,0:T(8,128)(2,1)S(1)}, bf16[16,9344]{1,0:T(8,128)(2,1)S(1)}, u32[]{:S(2)}, u32[]{:S(2)}) collective-permute-start(bf16[16,9344]{1,0:T(8,128)(2,1)S(1)} %get-tuple-element.40), channel_id=1, source_target_pairs={{0,8},{4,12},{8,0},{12,4},{1,9},{5,13},{9,1},{13,5},{2,10},{6,14},... | collective-permute-start | bytes 897032 | tf_op jit(solution)/shard_map/ppermute | solution.py:397
  278.5 37.1 %collective-permute-start.5 = (bf16[16,9344]{1,0:T(8,128)(2,1)S(1)}, bf16[16,9344]{1,0:T(8,128)(2,1)S(1)}, u32[]{:S(2)}, u32[]{:S(2)}) collective-permute-start(bf16[16,9344]{1,0:T(8,128)(2,1)S(1)} %get-tuple-element.41), channel_id=1, source_target_pairs={{0,12},{4,8},{8,4},{12,0},{1,13},{5,9},{9,5},{13,1},{2,14},{6,10},... | collective-permute-start | bytes 897032 | tf_op jit(solution)/shard_map/ppermute | solution.py:397
  (18 other events, 265.7 us)

commit v3 on v2

--- a/solution.py
+++ b/solution.py
@@ -16,7 +16,7 @@
 PAIR_LANES = 2 * NG
 ROWS = 16
 NEAR = 2
-UNROLL = 4
+UNROLL = 8
 
 PRECISE = lax.Precision.HIGHEST
 SPACING = 0.1348
@@ -282,9 +282,9 @@
 
 def column_scratch():
     return [
-        pltpu.VMEM((2, NG * ROWS, LANE), jnp.float32),
-        pltpu.VMEM((NG * ROWS, LANE), jnp.float32),
-        pltpu.VMEM((NG // 2 * ROWS, LANE), jnp.float32),
+        pltpu.VMEM((2, (NG + 1) * ROWS, LANE), jnp.float32),
+        pltpu.VMEM(((NG + 1) * ROWS, LANE), jnp.float32),
+        pltpu.VMEM(((NG // 2 + 1) * ROWS, LANE), jnp.float32),
     ]
 
 

time: 324 us -> 323 us (level)
  transfers between devices with their start and end apart: 18 -> 18, of which waited for: 6 -> 6; matrix products, arithmetic and copies ran while one was open for 6% -> 6% of each run, Pallas kernels for 25% -> 24%
where the time goes in v3:
time: 323 us
  waiting for transfers between devices  161 us (50%)
  Pallas kernels  93.5 us (29%)
  starting transfers between devices  32.1 us (10%)
  other arithmetic  15.7 us (5%)
  local copies, waits for them, and re-layouts  9.33 us (3%)
  blocking collectives  8.46 us (3%)
    ppermute x16, waiting for transfers between devices, exchange(): lax.ppermute(field, 'pen', [(i, i ^ s) for i in range(pen)])  161 us
    pallas_call x3, Pallas kernels, forward_planes(): pl.pallas_call(functools.partial(forward_kernel, slab, pen), out_shape=[n...  39.5 us
    pallas_call x3, Pallas kernels, inverse_planes(): pl.pallas_call(functools.partial(inverse_kernel, slab, pen, bool(part_row...  32.5 us
    ppermute x16, starting transfers between devices, exchange(): lax.ppermute(field, 'pen', [(i, i ^ s) for i in range(pen)])  24.2 us
    pallas_call x2, Pallas kernels, middle_columns(): pl.pallas_call(functools.partial(middle_kernel, pen, in_pieces, out_piece...  19.4 us
    div x1, other arithmetic, grid_weights(): return coulomb_kernel(square_sum, NG) / float(NG * NG * NG)  15.6 us
    all_to_all x1, blocking collectives, coulomb_part(): lax.all_to_all(shares, ('grp', 'blk'), split_axis=0, concat_axis=0, tiled...  8.46 us
    unnamed x48, local copies, waits for them, and re-layouts  8.07 us
  transfers between devices with their start and end apart: 18, of which 6 were waited for; matrix products, arithmetic and copies ran while one was open for 6% of the time, Pallas kernels for 24%

profile of v3, /device:TPU:8, one launch (start us, length us, event | category | flops | bytes accessed | tf_op | source)
XLA Modules:
  0.0 322.5 jit_solution(14775693440903992708)
XLA Ops:
  0.7 8.4 %forward_planes.3 = (bf16[48,9216]{1,0:T(8,128)(2,1)}, bf16[48,9216]{1,0:T(8,128)(2,1)}, bf16[16,9216]{1,0:T(8,128)(2,1)}, bf16[16,9216]{1,0:T(8,128)(2,1)}) custom-call(s32[2,2]{1,0:T(2,128)} %pairs_ref.11, bf16[8,48,36864]{2,1,0:T(8,128)(2,1)} %refs_4_.5, bf16[8,48,36864]{2,1,0:T(8,128)(2,1)} %refs_4_.5, ...), custom_call_target="tpu_custom_call" | custom-call | flops 1358954496 | bytes 3538944 | tf_op jit(solution)/shard_map/forward_planes/pallas_call | solution.py:300
  11.2 3.7 %all-to-all-start = ((bf16[4,32,128]{2,1,0:T(8,128)(2,1)}), bf16[4,32,128]{2,1,0:T(8,128)(2,1)S(1)}, u32[]{:S(2)}, u32[]{:S(2)}) async-start(bf16[4,32,128]{2,1,0:T(8,128)(2,1)} %broadcast_in_dim.76), calls=%async_computation | async-start | bytes 65536 | tf_op jit(solution)/shard_map/all_to_all | solution.py:560
  17.4 12.7 %forward_planes.4 = (bf16[48,9216]{1,0:T(8,128)(2,1)S(1)}, bf16[48,9216]{1,0:T(8,128)(2,1)}, bf16[32,9216]{1,0:T(8,128)(2,1)}, bf16[32,9216]{1,0:T(8,128)(2,1)}) custom-call(s32[2,2]{1,0:T(2,128)S(1)} %copy-done.14, bf16[8,48,36864]{2,1,0:T(8,128)(2,1)} %refs_4_.5, bf16[8,48,36864]{2,1,0:T(8,128)(2,1)} %refs_4_.5, ...), custom_call_target="tpu_custom_call", output_to_operand_aliasing={{0}: (5, {}), {1}: (6, {})} | custom-call | flops 2717908992 | bytes 7077888 | tf_op jit(solution)/shard_map/forward_planes/pallas_call | solution.py:300
  31.0 1.7 collective-permute-start.11
  38.1 4.2 %all-to-all-start.1 = ((f32[8,8,128]{2,1,0:T(8,128)}), f32[8,8,128]{2,1,0:T(8,128)S(1)}, u32[]{:S(2)}, u32[]{:S(2)}) async-start(f32[8,8,128]{2,1,0:T(8,128)} %broadcast_in_dim.77), calls=%async_computation.1 | async-start | bytes 65536 | tf_op jit(solution)/shard_map/all_to_all | solution.py:560
  42.3 15.6 %fusion.3.refs_0_.grid_ref = f32[104,9216]{1,0:T(8,128)} fusion(s32[9216]{0:T(1024)S(1)} %fusion.10, s32[104]{0:T(128)S(1)} %iota_multiply_fusion), kind=kLoop, calls=%fused_computation.5 | loop fusion | flops 9584640 | bytes 3871136 | tf_op jit(solution)/shard_map/div | solution.py:426
  60.3 18.4 %forward_planes.5 = (bf16[48,9216]{1,0:T(8,128)(2,1)}, bf16[48,9216]{1,0:T(8,128)(2,1)}, bf16[48,9216]{1,0:T(8,128)(2,1)}, bf16[48,9216]{1,0:T(8,128)(2,1)}) custom-call(s32[2,2]{1,0:T(2,128)} %pairs_ref.11, bf16[8,48,36864]{2,1,0:T(8,128)(2,1)} %refs_4_.5, bf16[8,48,36864]{2,1,0:T(8,128)(2,1)} %refs_4_.5, ...), custom_call_target="tpu_custom_call" | custom-call | flops 4076863488 | bytes 10616832 | tf_op jit(solution)/shard_map/forward_planes/pallas_call | solution.py:300
  78.8 2.8 collective-permute-start
  83.1 43.4 %collective-permute-done.10.refs_2_ = bf16[32,9216]{1,0:T(8,128)(2,1)} collective-permute-done((bf16[32,9216]{1,0:T(8,128)(2,1)}, bf16[32,9216]{1,0:T(8,128)(2,1)}, u32[]{:S(2)}, u32[]{:S(2)}) %collective-permute-start.10) | collective-permute-done | bytes 589856 | tf_op jit(solution)/shard_map/ppermute | solution.py:397
  126.6 10.1 %middle_columns.3 = (bf16[48,9216]{1,0:T(8,128)(2,1)S(1)}, bf16[48,9216]{1,0:T(8,128)(2,1)S(1)}, bf16[48,9216]{1,0:T(8,128)(2,1)}, bf16[48,9216]{1,0:T(8,128)(2,1)S(1)}) custom-call(bf16[384,192]{1,0:T(8,128)(2,1)S(1)} %copy-done.22, bf16[384,192]{1,0:T(8,128)(2,1)S(1)} %copy-done.21, f32[104,9216]{1,0:T(8,128)S(1)} %copy-done.2, ...), custom_call_target="tpu_custom_call" | custom-call | flops 3397386240 | bytes 14155776 | tf_op jit(solution)/shard_map/middle_columns/pallas_call | solution.py:341
  138.7 8.5 %all_to_all.15 = f32[8,16,128]{2,1,0:T(8,128)S(1)} all-to-all(f32[8,16,128]{2,1,0:T(8,128)S(1)} %bitcast.28), channel_id=1, replica_groups=mesh['grp'=2,'pen'=4,'blk'=4] {'grp','blk'}, dimensions={0} | all-to-all | bytes 131072 | tf_op jit(solution)/shard_map/all_to_all | solution.py:613
  147.2 3.3 %collective-permute-start.14 = (bf16[48,9216]{1,0:T(8,128)(2,1)}, bf16[48,9216]{1,0:T(8,128)(2,1)S(1)}, u32[]{:S(2)}, u32[]{:S(2)}) collective-permute-start(bf16[48,9216]{1,0:T(8,128)(2,1)} %copy-done.20), channel_id=1, source_target_pairs={{0,8},{4,12},{8,0},{12,4},{1,9},{5,13},{9,1},{13,5},{2,10},{6,14},... | collective-permute-start | bytes 2654216 | tf_op jit(solution)/shard_map/ppermute | solution.py:397
  150.8 50.9 %collective-permute-done.1.refs_1_ = bf16[48,9216]{1,0:T(8,128)(2,1)} collective-permute-done((bf16[48,9216]{1,0:T(8,128)(2,1)}, bf16[48,9216]{1,0:T(8,128)(2,1)}, u32[]{:S(2)}, u32[]{:S(2)}) %collective-permute-start.1) | collective-permute-done | bytes 884768 | tf_op jit(solution)/shard_map/ppermute | solution.py:397
  201.7 2.1 copy-done.3
  205.0 9.3 %middle_columns.2 = (bf16[32,9216]{1,0:T(8,128)(2,1)S(1)}, bf16[32,9216]{1,0:T(8,128)(2,1)S(1)}, bf16[16,9344]{1,0:T(8,128)(2,1)S(1)}, bf16[16,9344]{1,0:T(8,128...) custom-call(bf16[384,192]{1,0:T(8,128)(2,1)S(1)} %copy-done.22, bf16[384,192]{1,0:T(8,128)(2,1)S(1)} %copy-done.21, ...), custom_call_target="tpu_custom_call" | custom-call | flops 3397386240 | bytes 14155776 | tf_op jit(solution)/shard_map/middle_columns/pallas_call | solution.py:341
  214.3 2.3 collective-permute-start.3
  218.4 2.3 collective-permute-done.14.refs_2_
  220.7 3.3 %collective-permute-start.4 = (bf16[16,9344]{1,0:T(8,128)(2,1)S(1)}, bf16[16,9344]{1,0:T(8,128)(2,1)S(1)}, u32[]{:S(2)}, u32[]{:S(2)}) collective-permute-start(bf16[16,9344]{1,0:T(8,128)(2,1)S(1)} %get-tuple-element.40), channel_id=1, source_target_pairs={{0,8},{4,12},{8,0},{12,4},{1,9},{5,13},{9,1},{13,5},{2,10},{6,14},... | collective-permute-start | bytes 897032 | tf_op jit(solution)/shard_map/ppermute | solution.py:397
  224.0 54.4 %collective-permute-done.15.refs_3_ = bf16[48,9216]{1,0:T(8,128)(2,1)S(1)} collective-permute-done((bf16[48,9216]{1,0:T(8,128)(2,1)}, bf16[48,9216]{1,0:T(8,128)(2,1)S(1)}, u32[]{:S(2)}, u32[]{:S(2)}) %collective-permute-start.15) | collective-permute-done | bytes 884768 | tf_op jit(solution)/shard_map/ppermute | solution.py:397
  278.4 1.8 collective-permute-start.5
  280.2 14.7 %inverse_planes.3.refs_7_ = f32[2,48,36864]{2,1,0:T(8,128)} custom-call(s32[2,2]{1,0:T(2,128)S(1)} %copy-done.15, bf16[48,9216]{1,0:T(8,128)(2,1)S(1)} %get-tuple-element.48.refs_0_, bf16[48,9216]{1,0:T(8,128)(2,1)S(1)} %collective-permute-done.13.refs_1_, bf16[48,9216]{1,0:T(8,128)(2,1)S(1)} %collective-permute-done.14.refs_2_, ...), custom_call_target="tpu_custom_call" | custom-call | flops 3397386240 | bytes 14155776 | tf_op jit(solution)/shard_map/inverse_planes/pallas_call | solution.py:377
  294.8 8.8 %collective-permute-done.7.refs_3_ = bf16[32,9216]{1,0:T(8,128)(2,1)S(1)} collective-permute-done((bf16[32,9216]{1,0:T(8,128)(2,1)S(1)}, bf16[32,9216]{1,0:T(8,128)(2,1)S(1)}, u32[]{:S(2)}, u32[]{:S(2)}) %collective-permute-start.7) | collective-permute-done | bytes 589856 | tf_op jit(solution)/shard_map/ppermute | solution.py:397
  303.7 10.8 %inverse_planes.4.refs_7_ = f32[2,48,36864]{2,1,0:T(8,128)} custom-call(s32[2,2]{1,0:T(2,128)S(1)} %copy-done.15, bf16[48,9344]{1,0:T(8,128)(2,1)S(1)} %get-tuple-element.38.refs_0_, bf16[48,9344]{1,0:T(8,128)(2,1)S(1)} %collective-permute-done.3.refs_1_, bf16[32,9216]{1,0:T(8,128)(2,1)S(1)} %collective-permute-done.6.refs_2_, ...), custom_call_target="tpu_custom_call", output_to_operand_aliasing={{}: (8, {})} | custom-call | flops 2264924160 | bytes 9437184 | tf_op jit(solution)/shard_map/inverse_planes/pallas_call | solution.py:377
  315.5 7.0 %inverse_planes.5 = (f32[2,48,36864]{2,1,0:T(8,128)}, f32[4,128]{1,0:T(4,128)}) custom-call(s32[2,2]{1,0:T(2,128)S(1)} %copy-done.15, bf16[48,9344]{1,0:T(8,128)(2,1)S(1)} %get-tuple-element.38.refs_0_, bf16[48,9344]{1,0:T(8,128)(2,1)S(1)} %collective-permute-done.3.refs_1_, ...), custom_call_target="tpu_custom_call", output_to_operand_aliasing={{0}: (8, {})} | custom-call | flops 1132462080 | bytes 4718592 | tf_op jit(solution)/shard_map/inverse_planes/pallas_call | solution.py:377
  (90 shorter events, 20.5 us)
Async XLA Ops:
  9.0 72.5 %collective-permute-start.8 = (bf16[16,9216]{1,0:T(8,128)(2,1)}, bf16[16,9216]{1,0:T(8,128)(2,1)S(1)}, u32[]{:S(2)}, u32[]{:S(2)}) collective-permute-start(bf16[16,9216]{1,0:T(8,128)(2,1)} %get-tuple-element.32), channel_id=1, source_target_pairs={{0,12},{4,8},{8,4},{12,0},{1,13},{5,9},{9,5},{13,1},{2,14},{6,10},... | collective-permute-start | bytes 884744 | tf_op jit(solution)/shard_map/ppermute | solution.py:397
  11.2 25.0 %all-to-all-start = ((bf16[4,32,128]{2,1,0:T(8,128)(2,1)}), bf16[4,32,128]{2,1,0:T(8,128)(2,1)S(1)}, u32[]{:S(2)}, u32[]{:S(2)}) async-start(bf16[4,32,128]{2,1,0:T(8,128)(2,1)} %broadcast_in_dim.76), calls=%async_computation | async-start | bytes 65536 | tf_op jit(solution)/shard_map/all_to_all | solution.py:560
  15.0 63.8 %collective-permute-start.9 = (bf16[16,9216]{1,0:T(8,128)(2,1)}, bf16[16,9216]{1,0:T(8,128)(2,1)}, u32[]{:S(2)}, u32[]{:S(2)}) collective-permute-start(bf16[16,9216]{1,0:T(8,128)(2,1)} %get-tuple-element.44), channel_id=1, source_target_pairs={{0,8},{4,12},{8,0},{12,4},{1,9},{5,13},{9,1},{13,5},{2,10},{6,14},... | collective-permute-start | bytes 884744 | tf_op jit(solution)/shard_map/ppermute | solution.py:397
  31.0 50.6 %collective-permute-start.11 = (bf16[32,9216]{1,0:T(8,128)(2,1)}, bf16[32,9216]{1,0:T(8,128)(2,1)}, u32[]{:S(2)}, u32[]{:S(2)}) collective-permute-start(bf16[32,9216]{1,0:T(8,128)(2,1)} %get-tuple-element.45), channel_id=1, source_target_pairs={{0,8},{4,12},{8,0},{12,4},{1,9},{5,13},{9,1},{13,5},{2,10},{6,14},... | collective-permute-start | bytes 1769480 | tf_op jit(solution)/shard_map/ppermute | solution.py:397
  32.7 93.8 %collective-permute-start.10 = (bf16[32,9216]{1,0:T(8,128)(2,1)}, bf16[32,9216]{1,0:T(8,128)(2,1)}, u32[]{:S(2)}, u32[]{:S(2)}) collective-permute-start(bf16[32,9216]{1,0:T(8,128)(2,1)} %get-tuple-element.30), channel_id=1, source_target_pairs={{0,12},{4,8},{8,4},{12,0},{1,13},{5,9},{9,5},{13,1},{2,14},{6,10},... | collective-permute-start | bytes 1769480 | tf_op jit(solution)/shard_map/ppermute | solution.py:397
  33.7 92.8 %collective-permute-start.12 = (bf16[48,9216]{1,0:T(8,128)(2,1)}, bf16[48,9216]{1,0:T(8,128)(2,1)S(1)}, u32[]{:S(2)}, u32[]{:S(2)}) collective-permute-start(bf16[48,9216]{1,0:T(8,128)(2,1)} %get-tuple-element.46), channel_id=1, source_target_pairs={{0,4},{4,0},{8,12},{12,8},{1,5},{5,1},{9,13},{13,9},{2,6},{6,2},{1... | collective-permute-start | bytes 2654216 | tf_op jit(solution)/shard_map/ppermute | solution.py:397
  38.1 19.8 %all-to-all-start.1 = ((f32[8,8,128]{2,1,0:T(8,128)}), f32[8,8,128]{2,1,0:T(8,128)S(1)}, u32[]{:S(2)}, u32[]{:S(2)}) async-start(f32[8,8,128]{2,1,0:T(8,128)} %broadcast_in_dim.77), calls=%async_computation.1 | async-start | bytes 65536 | tf_op jit(solution)/shard_map/all_to_all | solution.py:560
  60.3 66.2 %copy-start.11 = (bf16[48,9216]{1,0:T(8,128)(2,1)S(1)}, bf16[48,9216]{1,0:T(8,128)(2,1)}, u32[]{:S(2)}) copy-start(bf16[48,9216]{1,0:T(8,128)(2,1)} %copy-done.10) | copy-start | bytes 2654212
  60.3 66.2 %copy-start.21 = (bf16[384,192]{1,0:T(8,128)(2,1)S(1)}, bf16[384,192]{1,0:T(8,128)(2,1)}, u32[]{:S(2)}) copy-start(bf16[384,192]{1,0:T(8,128)(2,1)} %constant.67.clone.out_table_ref) | copy-start | bytes 442372
  60.3 66.2 %copy-start.22 = (bf16[384,192]{1,0:T(8,128)(2,1)S(1)}, bf16[384,192]{1,0:T(8,128)(2,1)}, u32[]{:S(2)}) copy-start(bf16[384,192]{1,0:T(8,128)(2,1)} %constant.66.clone.in_ref) | copy-start | bytes 442372
  78.8 71.7 %collective-permute-start = (bf16[48,9216]{1,0:T(8,128)(2,1)}, bf16[48,9216]{1,0:T(8,128)(2,1)}, u32[]{:S(2)}, u32[]{:S(2)}) collective-permute-start(bf16[48,9216]{1,0:T(8,128)(2,1)} %get-tuple-element.34), channel_id=1, source_target_pairs={{0,12},{4,8},{8,4},{12,0},{1,13},{5,9},{9,5},{13,1},{2,14},{6,10},... | collective-permute-start | bytes 2654216 | tf_op jit(solution)/shard_map/ppermute | solution.py:397
  81.6 120.2 %collective-permute-start.1 = (bf16[48,9216]{1,0:T(8,128)(2,1)}, bf16[48,9216]{1,0:T(8,128)(2,1)}, u32[]{:S(2)}, u32[]{:S(2)}) collective-permute-start(bf16[48,9216]{1,0:T(8,128)(2,1)} %get-tuple-element.35), channel_id=1, source_target_pairs={{0,8},{4,12},{8,0},{12,4},{1,9},{5,13},{9,1},{13,5},{2,10},{6,14},... | collective-permute-start | bytes 2654216 | tf_op jit(solution)/shard_map/ppermute | solution.py:397
  81.6 120.1 %collective-permute-start.2 = (bf16[48,9216]{1,0:T(8,128)(2,1)}, bf16[48,9216]{1,0:T(8,128)(2,1)}, u32[]{:S(2)}, u32[]{:S(2)}) collective-permute-start(bf16[48,9216]{1,0:T(8,128)(2,1)} %get-tuple-element.36), channel_id=1, source_target_pairs={{0,4},{4,0},{8,12},{12,8},{1,5},{5,1},{9,13},{13,9},{2,6},{6,2},{1... | collective-permute-start | bytes 2654216 | tf_op jit(solution)/shard_map/ppermute | solution.py:397
  138.7 79.2 %collective-permute-start.13 = (bf16[48,9216]{1,0:T(8,128)(2,1)}, bf16[48,9216]{1,0:T(8,128)(2,1)S(1)}, u32[]{:S(2)}, u32[]{:S(2)}) collective-permute-start(bf16[48,9216]{1,0:T(8,128)(2,1)} %get-tuple-element.49), channel_id=1, source_target_pairs={{0,4},{4,0},{8,12},{12,8},{1,5},{5,1},{9,13},{13,9},{2,6},{6,2},{1... | collective-permute-start | bytes 2654216 | tf_op jit(solution)/shard_map/ppermute | solution.py:397
  147.2 73.5 %collective-permute-start.14 = (bf16[48,9216]{1,0:T(8,128)(2,1)}, bf16[48,9216]{1,0:T(8,128)(2,1)S(1)}, u32[]{:S(2)}, u32[]{:S(2)}) collective-permute-start(bf16[48,9216]{1,0:T(8,128)(2,1)} %copy-done.20), channel_id=1, source_target_pairs={{0,8},{4,12},{8,0},{12,4},{1,9},{5,13},{9,1},{13,5},{2,10},{6,14},... | collective-permute-start | bytes 2654216 | tf_op jit(solution)/shard_map/ppermute | solution.py:397
  150.5 127.9 %collective-permute-start.15 = (bf16[48,9216]{1,0:T(8,128)(2,1)}, bf16[48,9216]{1,0:T(8,128)(2,1)S(1)}, u32[]{:S(2)}, u32[]{:S(2)}) collective-permute-start(bf16[48,9216]{1,0:T(8,128)(2,1)} %copy-done.19), channel_id=1, source_target_pairs={{0,12},{4,8},{8,4},{12,0},{1,13},{5,9},{9,5},{13,1},{2,14},{6,10},... | collective-permute-start | bytes 2654216 | tf_op jit(solution)/shard_map/ppermute | solution.py:397
  205.0 75.2 %copy-start.4 = (bf16[2,2,256,256]{3,2,1,0:T(8,128)(2,1)S(1)}, bf16[2,2,256,256]{3,2,1,0:T(8,128)(2,1)}, u32[]{:S(2)}) copy-start(bf16[2,2,256,256]{3,2,1,0:T(8,128)(2,1)} %constant.63.clone.refs_6_) | copy-start | bytes 1572868
  205.0 75.2 %copy-start.7 = (bf16[384,192]{1,0:T(8,128)(2,1)S(1)}, bf16[384,192]{1,0:T(8,128)(2,1)}, u32[]{:S(2)}) copy-start(bf16[384,192]{1,0:T(8,128)(2,1)} %constant.65.clone.refs_5_) | copy-start | bytes 442372
  205.0 75.2 %copy-start.15 = (s32[2,2]{1,0:T(2,128)S(1)}, s32[2,2]{1,0:T(2,128)}, u32[]{:S(2)}) copy-start(s32[2,2]{1,0:T(2,128)} %pairs_ref.11) | copy-start | bytes 52
  214.3 89.4 %collective-permute-start.3 = (bf16[48,9344]{1,0:T(8,128)(2,1)S(1)}, bf16[48,9344]{1,0:T(8,128)(2,1)S(1)}, u32[]{:S(2)}, u32[]{:S(2)}) collective-permute-start(bf16[48,9344]{1,0:T(8,128)(2,1)S(1)} %get-tuple-element.39), channel_id=1, source_target_pairs={{0,4},{4,0},{8,12},{12,8},{1,5},{5,1},{9,13},{13,9},{2,6},{6,2},{1... | collective-permute-start | bytes 2691080 | tf_op jit(solution)/shard_map/ppermute | solution.py:397
  216.6 78.3 %collective-permute-start.6 = (bf16[32,9216]{1,0:T(8,128)(2,1)S(1)}, bf16[32,9216]{1,0:T(8,128)(2,1)S(1)}, u32[]{:S(2)}, u32[]{:S(2)}) collective-permute-start(bf16[32,9216]{1,0:T(8,128)(2,1)S(1)} %get-tuple-element.42), channel_id=1, source_target_pairs={{0,8},{4,12},{8,0},{12,4},{1,9},{5,13},{9,1},{13,5},{2,10},{6,14},... | collective-permute-start | bytes 1769480 | tf_op jit(solution)/shard_map/ppermute | solution.py:397
  217.9 85.8 %collective-permute-start.7 = (bf16[32,9216]{1,0:T(8,128)(2,1)S(1)}, bf16[32,9216]{1,0:T(8,128)(2,1)S(1)}, u32[]{:S(2)}, u32[]{:S(2)}) collective-permute-start(bf16[32,9216]{1,0:T(8,128)(2,1)S(1)} %get-tuple-element.43), channel_id=1, source_target_pairs={{0,12},{4,8},{8,4},{12,0},{1,13},{5,9},{9,5},{13,1},{2,14},{6,10},... | collective-permute-start | bytes 1769480 | tf_op jit(solution)/shard_map/ppermute | solution.py:397
  220.7 93.8 %collective-permute-start.4 = (bf16[16,9344]{1,0:T(8,128)(2,1)S(1)}, bf16[16,9344]{1,0:T(8,128)(2,1)S(1)}, u32[]{:S(2)}, u32[]{:S(2)}) collective-permute-start(bf16[16,9344]{1,0:T(8,128)(2,1)S(1)} %get-tuple-element.40), channel_id=1, source_target_pairs={{0,8},{4,12},{8,0},{12,4},{1,9},{5,13},{9,1},{13,5},{2,10},{6,14},... | collective-permute-start | bytes 897032 | tf_op jit(solution)/shard_map/ppermute | solution.py:397
  278.4 37.1 %collective-permute-start.5 = (bf16[16,9344]{1,0:T(8,128)(2,1)S(1)}, bf16[16,9344]{1,0:T(8,128)(2,1)S(1)}, u32[]{:S(2)}, u32[]{:S(2)}) collective-permute-start(bf16[16,9344]{1,0:T(8,128)(2,1)S(1)} %get-tuple-element.41), channel_id=1, source_target_pairs={{0,12},{4,8},{8,4},{12,0},{1,13},{5,9},{9,5},{13,1},{2,14},{6,10},... | collective-permute-start | bytes 897032 | tf_op jit(solution)/shard_map/ppermute | solution.py:397
  (18 other events, 263.7 us)

commit v4 on v3

--- a/solution.py
+++ b/solution.py
@@ -471,7 +471,7 @@
             )
             for s in range(NEAR, pen):
                 taken[s, first] = exchange(s, made[s], pen)
-            if p == 0 and first == 0:
+            if p == 0 and first + count == slab:
                 local = coulomb_local(made[-1])
         for s in range(NEAR):
             taken[s, 0] = exchange(s, made[s], pen)

time: 323 us -> 323 us (level)
  waiting for transfers between devices: 161 us -> 156 us
  local copies, waits for them, and re-layouts: 9.33 us -> 14.1 us
    ppermute x16, waiting for transfers between devices: 161 us -> 154 us  [exchange(): lax.ppermute(field, 'pen', [(i, i ^ s) for i in range(pen)])]
    unnamed x48 -> x60, local copies, waits for them, and re-layouts: 8.07 us -> 12.8 us
  transfers between devices with their start and end apart: 18 -> 18, of which waited for: 6 -> 8; matrix products, arithmetic and copies ran while one was open for 6% -> 6% of each run, Pallas kernels for 24% -> 24%
where the time goes in v4:
time: 323 us
  waiting for transfers between devices  156 us (48%)
  Pallas kernels  93.2 us (29%)
  starting transfers between devices  32.2 us (10%)
  other arithmetic  15.7 us (5%)
  local copies, waits for them, and re-layouts  14.1 us (4%)
  blocking collectives  8.46 us (3%)
    ppermute x16, waiting for transfers between devices, exchange(): lax.ppermute(field, 'pen', [(i, i ^ s) for i in range(pen)])  154 us
    pallas_call x3, Pallas kernels, forward_planes(): pl.pallas_call(functools.partial(forward_kernel, slab, pen), out_shape=[n...  39.3 us
    pallas_call x3, Pallas kernels, inverse_planes(): pl.pallas_call(functools.partial(inverse_kernel, slab, pen, bool(part_row...  32.5 us
    ppermute x16, starting transfers between devices, exchange(): lax.ppermute(field, 'pen', [(i, i ^ s) for i in range(pen)])  25 us
    pallas_call x2, Pallas kernels, middle_columns(): pl.pallas_call(functools.partial(middle_kernel, pen, in_pieces, out_piece...  19.3 us
    div x1, other arithmetic, grid_weights(): return coulomb_kernel(square_sum, NG) / float(NG * NG * NG)  15.6 us
    unnamed x60, local copies, waits for them, and re-layouts  12.8 us
    all_to_all x1, blocking collectives, coulomb_part(): lax.all_to_all(shares, ('grp', 'blk'), split_axis=0, concat_axis=0, tiled...  8.46 us
  transfers between devices with their start and end apart: 18, of which 8 were waited for; matrix products, arithmetic and copies ran while one was open for 6% of the time, Pallas kernels for 24%

profile of v4, /device:TPU:8, one launch (start us, length us, event | category | flops | bytes accessed | tf_op | source)
XLA Modules:
  0.0 322.6 jit_solution(13336489962881729259)
XLA Ops:
  0.7 8.4 %forward_planes.3 = (bf16[48,9216]{1,0:T(8,128)(2,1)}, bf16[48,9216]{1,0:T(8,128)(2,1)}, bf16[16,9216]{1,0:T(8,128)(2,1)}, bf16[16,9216]{1,0:T(8,128)(2,1)}) custom-call(s32[2,2]{1,0:T(2,128)} %pairs_ref.11, bf16[8,48,36864]{2,1,0:T(8,128)(2,1)} %refs_4_.5, bf16[8,48,36864]{2,1,0:T(8,128)(2,1)} %refs_4_.5, ...), custom_call_target="tpu_custom_call" | custom-call | flops 1358954496 | bytes 3538944 | tf_op jit(solution)/shard_map/forward_planes/pallas_call | solution.py:300
  14.0 12.6 %forward_planes.4 = (bf16[48,9216]{1,0:T(8,128)(2,1)S(1)}, bf16[48,9216]{1,0:T(8,128)(2,1)S(1)}, bf16[32,9216]{1,0:T(8,128)(2,1)}, bf16[32,9216]{1,0:T(8,128)(2,1)}) custom-call(s32[2,2]{1,0:T(2,128)S(1)} %copy-done.16, bf16[8,48,36864]{2,1,0:T(8,128)(2,1)} %refs_4_.5, bf16[8,48,36864]{2,1,0:T(8,128)(2,1)} %refs_4_.5, ...), custom_call_target="tpu_custom_call", output_to_operand_aliasing={{0}: (5, {}), {1}: (6, {})} | custom-call | flops 2717908992 | bytes 7077888 | tf_op jit(solution)/shard_map/forward_planes/pallas_call | solution.py:300
  28.5 2.9 collective-permute-start.10
  32.0 3.7 %all-to-all-start = ((bf16[4,32,128]{2,1,0:T(8,128)(2,1)}), bf16[4,32,128]{2,1,0:T(8,128)(2,1)S(1)}, u32[]{:S(2)}, u32[]{:S(2)}) async-start(bf16[4,32,128]{2,1,0:T(8,128)(2,1)} %broadcast_in_dim.76), calls=%async_computation | async-start | bytes 65536 | tf_op jit(solution)/shard_map/all_to_all | solution.py:560
  38.0 2.5 all-to-all-done
  42.3 3.5 %all-to-all-start.1 = ((f32[8,8,128]{2,1,0:T(8,128)}), f32[8,8,128]{2,1,0:T(8,128)S(1)}, u32[]{:S(2)}, u32[]{:S(2)}) async-start(f32[8,8,128]{2,1,0:T(8,128)} %broadcast_in_dim.77), calls=%async_computation.1 | async-start | bytes 65536 | tf_op jit(solution)/shard_map/all_to_all | solution.py:560
  45.9 15.6 %fusion.3.refs_0_.grid_ref = f32[104,9216]{1,0:T(8,128)} fusion(s32[9216]{0:T(1024)S(1)} %fusion.10, s32[104]{0:T(128)S(1)} %iota_multiply_fusion), kind=kLoop, calls=%fused_computation.5 | loop fusion | flops 9584640 | bytes 3871136 | tf_op jit(solution)/shard_map/div | solution.py:426
  64.0 18.4 %forward_planes.5 = (bf16[48,9216]{1,0:T(8,128)(2,1)}, bf16[48,9216]{1,0:T(8,128)(2,1)}, bf16[48,9216]{1,0:T(8,128)(2,1)}, bf16[48,9216]{1,0:T(8,128)(2,1)}) custom-call(s32[2,2]{1,0:T(2,128)} %pairs_ref.11, bf16[8,48,36864]{2,1,0:T(8,128)(2,1)} %refs_4_.5, bf16[8,48,36864]{2,1,0:T(8,128)(2,1)} %refs_4_.5, ...), custom_call_target="tpu_custom_call" | custom-call | flops 4076863488 | bytes 10616832 | tf_op jit(solution)/shard_map/forward_planes/pallas_call | solution.py:300
  82.7 2.6 collective-permute-start.1
  85.3 40.6 %collective-permute-done.11.refs_3_ = bf16[32,9216]{1,0:T(8,128)(2,1)} collective-permute-done((bf16[32,9216]{1,0:T(8,128)(2,1)}, bf16[32,9216]{1,0:T(8,128)(2,1)}, u32[]{:S(2)}, u32[]{:S(2)}) %collective-permute-start.11) | collective-permute-done | bytes 589856 | tf_op jit(solution)/shard_map/ppermute | solution.py:397
  130.0 10.0 %middle_columns.3 = (bf16[48,9216]{1,0:T(8,128)(2,1)S(1)}, bf16[48,9216]{1,0:T(8,128)(2,1)S(1)}, bf16[48,9216]{1,0:T(8,128)(2,1)}, bf16[48,9216]{1,0:T(8,128)(2,1)S(1)}) custom-call(bf16[384,192]{1,0:T(8,128)(2,1)S(1)} %copy-done.27, bf16[384,192]{1,0:T(8,128)(2,1)S(1)} %copy-done.25, f32[104,9216]{1,0:T(8,128)S(1)} %copy-done.2, ...), custom_call_target="tpu_custom_call" | custom-call | flops 3397386240 | bytes 14155776 | tf_op jit(solution)/shard_map/middle_columns/pallas_call | solution.py:341
  142.1 8.5 %all_to_all.15 = f32[8,16,128]{2,1,0:T(8,128)S(1)} all-to-all(f32[8,16,128]{2,1,0:T(8,128)S(1)} %bitcast.28), channel_id=1, replica_groups=mesh['grp'=2,'pen'=4,'blk'=4] {'grp','blk'}, dimensions={0} | all-to-all | bytes 131072 | tf_op jit(solution)/shard_map/all_to_all | solution.py:613
  150.6 3.3 %collective-permute-start.14 = (bf16[48,9216]{1,0:T(8,128)(2,1)}, bf16[48,9216]{1,0:T(8,128)(2,1)S(1)}, u32[]{:S(2)}, u32[]{:S(2)}) collective-permute-start(bf16[48,9216]{1,0:T(8,128)(2,1)} %copy-done.22), channel_id=1, source_target_pairs={{0,8},{4,12},{8,0},{12,4},{1,9},{5,13},{9,1},{13,5},{2,10},{6,14},... | collective-permute-start | bytes 2654216 | tf_op jit(solution)/shard_map/ppermute | solution.py:397
  154.1 11.4 %collective-permute-done.1.refs_1_ = bf16[48,9216]{1,0:T(8,128)(2,1)} collective-permute-done((bf16[48,9216]{1,0:T(8,128)(2,1)}, bf16[48,9216]{1,0:T(8,128)(2,1)}, u32[]{:S(2)}, u32[]{:S(2)}) %collective-permute-start.1) | collective-permute-done | bytes 884768 | tf_op jit(solution)/shard_map/ppermute | solution.py:397
  165.5 4.7 %collective-permute-done.2.refs_2_ = bf16[48,9216]{1,0:T(8,128)(2,1)} collective-permute-done((bf16[48,9216]{1,0:T(8,128)(2,1)}, bf16[48,9216]{1,0:T(8,128)(2,1)}, u32[]{:S(2)}, u32[]{:S(2)}) %collective-permute-start.2) | collective-permute-done | bytes 884768 | tf_op jit(solution)/shard_map/ppermute | solution.py:397
  174.1 9.3 %middle_columns.2 = (bf16[32,9216]{1,0:T(8,128)(2,1)S(1)}, bf16[32,9216]{1,0:T(8,128)(2,1)S(1)}, bf16[16,9344]{1,0:T(8,128)(2,1)S(1)}, bf16[16,9344]{1,0:T(8,128...) custom-call(bf16[384,192]{1,0:T(8,128)(2,1)S(1)} %copy-done.28, bf16[384,192]{1,0:T(8,128)(2,1)S(1)} %copy-done.26, ...), custom_call_target="tpu_custom_call" | custom-call | flops 3397386240 | bytes 14155776 | tf_op jit(solution)/shard_map/middle_columns/pallas_call | solution.py:341
  183.4 2.6 collective-permute-start.3
  186.2 38.1 %collective-permute-done.13.refs_1_ = bf16[48,9216]{1,0:T(8,128)(2,1)S(1)} collective-permute-done((bf16[48,9216]{1,0:T(8,128)(2,1)}, bf16[48,9216]{1,0:T(8,128)(2,1)S(1)}, u32[]{:S(2)}, u32[]{:S(2)}) %collective-permute-start.13) | collective-permute-done | bytes 884768 | tf_op jit(solution)/shard_map/ppermute | solution.py:397
  226.1 3.0 collective-permute-start.4
  229.1 49.4 %collective-permute-done.15.refs_3_ = bf16[48,9216]{1,0:T(8,128)(2,1)S(1)} collective-permute-done((bf16[48,9216]{1,0:T(8,128)(2,1)}, bf16[48,9216]{1,0:T(8,128)(2,1)S(1)}, u32[]{:S(2)}, u32[]{:S(2)}) %collective-permute-start.15) | collective-permute-done | bytes 884768 | tf_op jit(solution)/shard_map/ppermute | solution.py:397
  280.2 14.6 %inverse_planes.3.refs_7_ = f32[2,48,36864]{2,1,0:T(8,128)} custom-call(s32[2,2]{1,0:T(2,128)S(1)} %copy-done.17, bf16[48,9216]{1,0:T(8,128)(2,1)S(1)} %get-tuple-element.48.refs_0_, bf16[48,9216]{1,0:T(8,128)(2,1)S(1)} %collective-permute-done.13.refs_1_, bf16[48,9216]{1,0:T(8,128)(2,1)S(1)} %collective-permute-done.14.refs_2_, ...), custom_call_target="tpu_custom_call" | custom-call | flops 3397386240 | bytes 14155776 | tf_op jit(solution)/shard_map/inverse_planes/pallas_call | solution.py:377
  294.9 8.9 %collective-permute-done.7.refs_3_ = bf16[32,9216]{1,0:T(8,128)(2,1)S(1)} collective-permute-done((bf16[32,9216]{1,0:T(8,128)(2,1)S(1)}, bf16[32,9216]{1,0:T(8,128)(2,1)S(1)}, u32[]{:S(2)}, u32[]{:S(2)}) %collective-permute-start.7) | collective-permute-done | bytes 589856 | tf_op jit(solution)/shard_map/ppermute | solution.py:397
  303.7 10.8 %inverse_planes.4.refs_7_ = f32[2,48,36864]{2,1,0:T(8,128)} custom-call(s32[2,2]{1,0:T(2,128)S(1)} %copy-done.17, bf16[48,9344]{1,0:T(8,128)(2,1)S(1)} %get-tuple-element.37.refs_0_, bf16[48,9344]{1,0:T(8,128)(2,1)S(1)} %collective-permute-done.3.refs_1_, bf16[32,9216]{1,0:T(8,128)(2,1)S(1)} %collective-permute-done.6.refs_2_, ...), custom_call_target="tpu_custom_call", output_to_operand_aliasing={{}: (8, {})} | custom-call | flops 2264924160 | bytes 9437184 | tf_op jit(solution)/shard_map/inverse_planes/pallas_call | solution.py:377
  315.6 7.0 %inverse_planes.5 = (f32[2,48,36864]{2,1,0:T(8,128)}, f32[4,128]{1,0:T(4,128)}) custom-call(s32[2,2]{1,0:T(2,128)S(1)} %copy-done.17, bf16[48,9344]{1,0:T(8,128)(2,1)S(1)} %get-tuple-element.37.refs_0_, bf16[48,9344]{1,0:T(8,128)(2,1)S(1)} %collective-permute-done.3.refs_1_, ...), custom_call_target="tpu_custom_call", output_to_operand_aliasing={{0}: (8, {})} | custom-call | flops 1132462080 | bytes 4718592 | tf_op jit(solution)/shard_map/inverse_planes/pallas_call | solution.py:377
  (102 shorter events, 29.0 us)
Async XLA Ops:
  9.0 73.3 %collective-permute-start.8 = (bf16[16,9216]{1,0:T(8,128)(2,1)}, bf16[16,9216]{1,0:T(8,128)(2,1)S(1)}, u32[]{:S(2)}, u32[]{:S(2)}) collective-permute-start(bf16[16,9216]{1,0:T(8,128)(2,1)} %get-tuple-element.43), channel_id=1, source_target_pairs={{0,12},{4,8},{8,4},{12,0},{1,13},{5,9},{9,5},{13,1},{2,14},{6,10},... | collective-permute-start | bytes 884744 | tf_op jit(solution)/shard_map/ppermute | solution.py:397
  10.6 72.1 %collective-permute-start.9 = (bf16[16,9216]{1,0:T(8,128)(2,1)}, bf16[16,9216]{1,0:T(8,128)(2,1)}, u32[]{:S(2)}, u32[]{:S(2)}) collective-permute-start(bf16[16,9216]{1,0:T(8,128)(2,1)} %get-tuple-element.44), channel_id=1, source_target_pairs={{0,8},{4,12},{8,0},{12,4},{1,9},{5,13},{9,1},{13,5},{2,10},{6,14},... | collective-permute-start | bytes 884744 | tf_op jit(solution)/shard_map/ppermute | solution.py:397
  28.5 99.6 %collective-permute-start.10 = (bf16[32,9216]{1,0:T(8,128)(2,1)}, bf16[32,9216]{1,0:T(8,128)(2,1)S(1)}, u32[]{:S(2)}, u32[]{:S(2)}) collective-permute-start(bf16[32,9216]{1,0:T(8,128)(2,1)} %get-tuple-element.30), channel_id=1, source_target_pairs={{0,12},{4,8},{8,4},{12,0},{1,13},{5,9},{9,5},{13,1},{2,14},{6,10},... | collective-permute-start | bytes 1769480 | tf_op jit(solution)/shard_map/ppermute | solution.py:397
  32.0 8.5 %all-to-all-start = ((bf16[4,32,128]{2,1,0:T(8,128)(2,1)}), bf16[4,32,128]{2,1,0:T(8,128)(2,1)S(1)}, u32[]{:S(2)}, u32[]{:S(2)}) async-start(bf16[4,32,128]{2,1,0:T(8,128)(2,1)} %broadcast_in_dim.76), calls=%async_computation | async-start | bytes 65536 | tf_op jit(solution)/shard_map/all_to_all | solution.py:560
  35.8 90.1 %collective-permute-start.11 = (bf16[32,9216]{1,0:T(8,128)(2,1)}, bf16[32,9216]{1,0:T(8,128)(2,1)}, u32[]{:S(2)}, u32[]{:S(2)}) collective-permute-start(bf16[32,9216]{1,0:T(8,128)(2,1)} %get-tuple-element.45), channel_id=1, source_target_pairs={{0,8},{4,12},{8,0},{12,4},{1,9},{5,13},{9,1},{13,5},{2,10},{6,14},... | collective-permute-start | bytes 1769480 | tf_op jit(solution)/shard_map/ppermute | solution.py:397
  36.7 92.2 %collective-permute-start.12 = (bf16[48,9216]{1,0:T(8,128)(2,1)}, bf16[48,9216]{1,0:T(8,128)(2,1)S(1)}, u32[]{:S(2)}, u32[]{:S(2)}) collective-permute-start(bf16[48,9216]{1,0:T(8,128)(2,1)} %copy-done.13), channel_id=1, source_target_pairs={{0,4},{4,0},{8,12},{12,8},{1,5},{5,1},{9,13},{13,9},{2,6},{6,2},{1... | collective-permute-start | bytes 2654216 | tf_op jit(solution)/shard_map/ppermute | solution.py:397
  42.3 19.1 %all-to-all-start.1 = ((f32[8,8,128]{2,1,0:T(8,128)}), f32[8,8,128]{2,1,0:T(8,128)S(1)}, u32[]{:S(2)}, u32[]{:S(2)}) async-start(f32[8,8,128]{2,1,0:T(8,128)} %broadcast_in_dim.77), calls=%async_computation.1 | async-start | bytes 65536 | tf_op jit(solution)/shard_map/all_to_all | solution.py:560
  64.0 64.9 %copy-start.11 = (bf16[48,9216]{1,0:T(8,128)(2,1)S(1)}, bf16[48,9216]{1,0:T(8,128)(2,1)}, u32[]{:S(2)}) copy-start(bf16[48,9216]{1,0:T(8,128)(2,1)} %copy-done.10) | copy-start | bytes 2654212
  64.0 64.9 %copy-start.25 = (bf16[384,192]{1,0:T(8,128)(2,1)S(1)}, bf16[384,192]{1,0:T(8,128)(2,1)}, u32[]{:S(2)}) copy-start(bf16[384,192]{1,0:T(8,128)(2,1)} %constant.67.clone.out_table_ref) | copy-start | bytes 442372
  64.0 65.0 %copy-start.27 = (bf16[384,192]{1,0:T(8,128)(2,1)S(1)}, bf16[384,192]{1,0:T(8,128)(2,1)}, u32[]{:S(2)}) copy-start(bf16[384,192]{1,0:T(8,128)(2,1)} %constant.66.clone.in_ref) | copy-start | bytes 442372
  82.4 71.5 %collective-permute-start = (bf16[48,9216]{1,0:T(8,128)(2,1)}, bf16[48,9216]{1,0:T(8,128)(2,1)}, u32[]{:S(2)}, u32[]{:S(2)}) collective-permute-start(bf16[48,9216]{1,0:T(8,128)(2,1)} %get-tuple-element.33), channel_id=1, source_target_pairs={{0,12},{4,8},{8,4},{12,0},{1,13},{5,9},{9,5},{13,1},{2,14},{6,10},... | collective-permute-start | bytes 2654216 | tf_op jit(solution)/shard_map/ppermute | solution.py:397
  82.7 82.8 %collective-permute-start.1 = (bf16[48,9216]{1,0:T(8,128)(2,1)}, bf16[48,9216]{1,0:T(8,128)(2,1)}, u32[]{:S(2)}, u32[]{:S(2)}) collective-permute-start(bf16[48,9216]{1,0:T(8,128)(2,1)} %get-tuple-element.34), channel_id=1, source_target_pairs={{0,8},{4,12},{8,0},{12,4},{1,9},{5,13},{9,1},{13,5},{2,10},{6,14},... | collective-permute-start | bytes 2654216 | tf_op jit(solution)/shard_map/ppermute | solution.py:397
  125.9 44.2 %collective-permute-start.2 = (bf16[48,9216]{1,0:T(8,128)(2,1)}, bf16[48,9216]{1,0:T(8,128)(2,1)}, u32[]{:S(2)}, u32[]{:S(2)}) collective-permute-start(bf16[48,9216]{1,0:T(8,128)(2,1)} %get-tuple-element.35), channel_id=1, source_target_pairs={{0,4},{4,0},{8,12},{12,8},{1,5},{5,1},{9,13},{13,9},{2,6},{6,2},{1... | collective-permute-start | bytes 2654216 | tf_op jit(solution)/shard_map/ppermute | solution.py:397
  142.1 82.3 %collective-permute-start.13 = (bf16[48,9216]{1,0:T(8,128)(2,1)}, bf16[48,9216]{1,0:T(8,128)(2,1)S(1)}, u32[]{:S(2)}, u32[]{:S(2)}) collective-permute-start(bf16[48,9216]{1,0:T(8,128)(2,1)} %get-tuple-element.49), channel_id=1, source_target_pairs={{0,4},{4,0},{8,12},{12,8},{1,5},{5,1},{9,13},{13,9},{2,6},{6,2},{1... | collective-permute-start | bytes 2654216 | tf_op jit(solution)/shard_map/ppermute | solution.py:397
  150.6 75.5 %collective-permute-start.14 = (bf16[48,9216]{1,0:T(8,128)(2,1)}, bf16[48,9216]{1,0:T(8,128)(2,1)S(1)}, u32[]{:S(2)}, u32[]{:S(2)}) collective-permute-start(bf16[48,9216]{1,0:T(8,128)(2,1)} %copy-done.22), channel_id=1, source_target_pairs={{0,8},{4,12},{8,0},{12,4},{1,9},{5,13},{9,1},{13,5},{2,10},{6,14},... | collective-permute-start | bytes 2654216 | tf_op jit(solution)/shard_map/ppermute | solution.py:397
  153.9 124.6 %collective-permute-start.15 = (bf16[48,9216]{1,0:T(8,128)(2,1)}, bf16[48,9216]{1,0:T(8,128)(2,1)S(1)}, u32[]{:S(2)}, u32[]{:S(2)}) collective-permute-start(bf16[48,9216]{1,0:T(8,128)(2,1)} %copy-done.21), channel_id=1, source_target_pairs={{0,12},{4,8},{8,4},{12,0},{1,13},{5,9},{9,5},{13,1},{2,14},{6,10},... | collective-permute-start | bytes 2654216 | tf_op jit(solution)/shard_map/ppermute | solution.py:397
  174.1 106.1 %copy-start.4 = (bf16[2,2,256,256]{3,2,1,0:T(8,128)(2,1)S(1)}, bf16[2,2,256,256]{3,2,1,0:T(8,128)(2,1)}, u32[]{:S(2)}) copy-start(bf16[2,2,256,256]{3,2,1,0:T(8,128)(2,1)} %constant.63.clone.refs_6_) | copy-start | bytes 1572868
  174.1 106.1 %copy-start.7 = (bf16[384,192]{1,0:T(8,128)(2,1)S(1)}, bf16[384,192]{1,0:T(8,128)(2,1)}, u32[]{:S(2)}) copy-start(bf16[384,192]{1,0:T(8,128)(2,1)} %constant.65.clone.refs_5_) | copy-start | bytes 442372
  174.1 106.1 %copy-start.17 = (s32[2,2]{1,0:T(2,128)S(1)}, s32[2,2]{1,0:T(2,128)}, u32[]{:S(2)}) copy-start(s32[2,2]{1,0:T(2,128)} %pairs_ref.11) | copy-start | bytes 52
  183.4 120.4 %collective-permute-start.3 = (bf16[48,9344]{1,0:T(8,128)(2,1)S(1)}, bf16[48,9344]{1,0:T(8,128)(2,1)S(1)}, u32[]{:S(2)}, u32[]{:S(2)}) collective-permute-start(bf16[48,9344]{1,0:T(8,128)(2,1)S(1)} %get-tuple-element.38), channel_id=1, source_target_pairs={{0,4},{4,0},{8,12},{12,8},{1,5},{5,1},{9,13},{13,9},{2,6},{6,2},{1... | collective-permute-start | bytes 2691080 | tf_op jit(solution)/shard_map/ppermute | solution.py:397
  185.9 108.9 %collective-permute-start.6 = (bf16[32,9216]{1,0:T(8,128)(2,1)S(1)}, bf16[32,9216]{1,0:T(8,128)(2,1)S(1)}, u32[]{:S(2)}, u32[]{:S(2)}) collective-permute-start(bf16[32,9216]{1,0:T(8,128)(2,1)S(1)} %get-tuple-element.41), channel_id=1, source_target_pairs={{0,8},{4,12},{8,0},{12,4},{1,9},{5,13},{9,1},{13,5},{2,10},{6,14},... | collective-permute-start | bytes 1769480 | tf_op jit(solution)/shard_map/ppermute | solution.py:397
  224.3 79.4 %collective-permute-start.7 = (bf16[32,9216]{1,0:T(8,128)(2,1)S(1)}, bf16[32,9216]{1,0:T(8,128)(2,1)S(1)}, u32[]{:S(2)}, u32[]{:S(2)}) collective-permute-start(bf16[32,9216]{1,0:T(8,128)(2,1)S(1)} %get-tuple-element.42), channel_id=1, source_target_pairs={{0,12},{4,8},{8,4},{12,0},{1,13},{5,9},{9,5},{13,1},{2,14},{6,10},... | collective-permute-start | bytes 1769480 | tf_op jit(solution)/shard_map/ppermute | solution.py:397
  226.1 88.5 %collective-permute-start.4 = (bf16[16,9344]{1,0:T(8,128)(2,1)S(1)}, bf16[16,9344]{1,0:T(8,128)(2,1)S(1)}, u32[]{:S(2)}, u32[]{:S(2)}) collective-permute-start(bf16[16,9344]{1,0:T(8,128)(2,1)S(1)} %get-tuple-element.39), channel_id=1, source_target_pairs={{0,8},{4,12},{8,0},{12,4},{1,9},{5,13},{9,1},{13,5},{2,10},{6,14},... | collective-permute-start | bytes 897032 | tf_op jit(solution)/shard_map/ppermute | solution.py:397
  278.4 37.1 %collective-permute-start.5 = (bf16[16,9344]{1,0:T(8,128)(2,1)S(1)}, bf16[16,9344]{1,0:T(8,128)(2,1)S(1)}, u32[]{:S(2)}, u32[]{:S(2)}) collective-permute-start(bf16[16,9344]{1,0:T(8,128)(2,1)S(1)} %get-tuple-element.40), channel_id=1, source_target_pairs={{0,12},{4,8},{8,4},{12,0},{1,13},{5,9},{9,5},{13,1},{2,14},{6,10},... | collective-permute-start | bytes 897032 | tf_op jit(solution)/shard_map/ppermute | solution.py:397
  (24 other events, 327.7 us)
